TPU v7x, 256 devices: a whole 4x4x8 slice. The times are simulated.
256 devices in a mesh: grp: 2 (over y_hi), band: 16 (over x, y_lo, core), ga: 8 (over z).
Axes of the slice: x: 4, y: 4 (y_hi: 2, y_lo: 2; y = y_hi * 2 + y_lo), z: 8, core: 2. Of those that a mesh axis runs over, the one named last changes fastest.
Arguments:
- occupied: bfloat16 [128, 192, 192], P(('grp', 'band'), 'ga'), may hold values from -4 to 4
- response: bfloat16 [128, 192, 192], P('band', 'ga'), may hold values from -10 to 10
- ground_state: bfloat16 [128, 192, 192], P('band', 'ga'), may hold values from -4 to 4
- field_index: int32 [128], P('band'), may hold values from 0 to 2
- band_energy: float32 [128], P('band'), may hold values from -2 to -0.2
- local_potential: float32 [192, 192], P('ga'), may hold values from -1.5 to 1.5
- field_potential: float32 [3, 192, 192], P(None, 'ga'), may hold values from -6 to 6
- kernel_table: float32 [192, 192], P(None, 'ga'), may hold values from 0.01 to 10
Outputs:
- projector: bfloat16 [128, 192, 192], P('band', 'ga')
- residual: float32 [128, 192, 192], P('band', 'ga')
All inputs are finite; a program needn't handle non-finite values.
Results may differ from a plain program's by a relative error of at most 0.006.
Values may be sent and summed in bfloat16 or wider, within the bound.
A program may use at most 64 MiB of HBM per device.

v0:
```python
import jax
import jax.numpy as jnp
from jax import lax
from jax.sharding import PartitionSpec as P

EXCHANGE_FRACTION = 0.25


def passed_along(x, axis, by):
    devices = lax.axis_size(axis)
    return lax.ppermute(x, axis, [(i, (i + by) % devices) for i in range(devices)])


def padded_2(block, sides, width):
    for axis, dim in sides:
        count = lax.axis_size(axis)
        forward = [(i, i + 1) for i in range(count - 1)]
        forward.append((count - 1, 0))
        backward = [(target, source) for source, target in forward]
        low = lax.ppermute(
            lax.slice_in_dim(block, block.shape[dim] - width, None, axis=dim), axis, forward
        )
        high = lax.ppermute(lax.slice_in_dim(block, 0, width, axis=dim), axis, backward)
        block = jnp.concatenate([low, block, high], axis=dim)
    return block


def cosine_table(length):
    rows = lax.broadcasted_iota(jnp.float32, (length, length), 0)
    cols = lax.broadcasted_iota(jnp.float32, (length, length), 1)
    factor = jnp.where(rows == 0, jnp.sqrt(1.0 / length), jnp.sqrt(2.0 / length)).astype(
        jnp.float32
    )
    return (factor * jnp.cos(jnp.pi * (cols + 0.5) * rows / length)).astype(jnp.bfloat16)


def pair_field(block_now, response, table_one, table_two, kernel_local, occ_count):
    block_f32 = block_now.astype(jnp.float32)
    density = (block_f32[:, None] * response.astype(jnp.float32)[None]).astype(jnp.bfloat16)
    count_occ, count_resp, rows, cols = density.shape
    density = density.reshape(count_occ * count_resp, rows, cols)
    first = jnp.einsum(
        "pan,kn->pak", density, table_two, preferred_element_type=jnp.float32
    ).astype(jnp.bfloat16)
    second = jnp.einsum(
        "ka,pab->pkb",
        table_one,
        lax.all_to_all(first, "ga", split_axis=2, concat_axis=1, tiled=True),
        preferred_element_type=jnp.float32,
    )
    weighted = (second * kernel_local).astype(jnp.bfloat16)
    third = jnp.einsum(
        "ka,pkb->pab", table_one, weighted, preferred_element_type=jnp.float32
    ).astype(jnp.bfloat16)
    returned = lax.all_to_all(third, "ga", split_axis=1, concat_axis=2, tiled=True)
    potential = jnp.einsum("pak,kn->pan", returned, table_two, preferred_element_type=jnp.float32)
    potential = potential.reshape(count_occ, count_resp, rows, cols)
    return jnp.sum(block_f32[:, None] * potential, axis=0) / occ_count


def on_device(
    occupied,
    response,
    ground_state,
    field_index,
    band_energy,
    local_potential,
    field_potential,
    kernel_table,
):
    n_band = lax.axis_size("band")
    occ_count = occupied.shape[0] * lax.axis_size("grp") * n_band
    resp_count, slab_rows, grid_cols = response.shape
    grid_rows = kernel_table.shape[0]
    table_one = cosine_table(grid_rows)
    table_two = cosine_table(grid_cols)
    start_total = jnp.zeros(response.shape, jnp.float32)

    def cycle_turn(step, carry):
        block_now, total = carry
        total = total + pair_field(
            block_now, response, table_one, table_two, kernel_table, occ_count
        )
        block_now = passed_along(block_now, "band", 1)
        return (block_now, total)

    last_block, total = lax.fori_loop(0, n_band - 1, cycle_turn, (occupied, start_total))
    total = total + pair_field(last_block, response, table_one, table_two, kernel_table, occ_count)
    exchange = lax.psum(total, "grp")
    exchange_round = exchange.astype(jnp.bfloat16)
    position = lax.axis_index("band")
    grid_count = grid_rows * grid_cols
    partial_value = (
        jnp.einsum(
            "rab,sab->rs",
            lax.all_gather(response, "band", axis=0, tiled=True),
            exchange_round,
            preferred_element_type=jnp.float32,
        )
        / grid_count
    )
    all_resp = partial_value.shape[0]
    partial_value = lax.psum(partial_value, "ga")
    gram = lax.all_gather(partial_value, "band", axis=1, tiled=True)
    gram = 0.5 * (gram + gram.T)
    lower_factor = jnp.linalg.cholesky(gram)
    inverse = lax.linalg.triangular_solve(
        lower_factor, jnp.eye(all_resp, dtype=jnp.float32), left_side=True, lower=True
    )
    my_rows = lax.dynamic_slice_in_dim(inverse, position * resp_count, resp_count, 0)
    piece = lax.all_gather(exchange_round, "band", axis=0, tiled=True)
    flat_piece = piece.reshape(piece.shape[0], -1).astype(jnp.float32)
    projected = jnp.dot(my_rows, flat_piece, precision=lax.Precision.HIGHEST)
    projector = projected.reshape(resp_count, slab_rows, grid_cols).astype(jnp.bfloat16)
    padded = padded_2(response, (("ga", 1),), 1)
    resp_f32 = response.astype(jnp.float32)
    neighbours = padded[:, 2:].astype(jnp.float32) + padded[:, :-2].astype(jnp.float32)
    neighbours = neighbours + jnp.roll(resp_f32, 1, axis=2) + jnp.roll(resp_f32, -1, axis=2)
    kinetic = 0.5 * (4.0 * resp_f32 - neighbours)
    field_count = field_potential.shape[0]
    select = (field_index[:, None] == jnp.arange(field_count, dtype=jnp.int32)[None]).astype(
        jnp.float32
    )
    perturb = jnp.einsum("rf,fab->rab", select, field_potential, precision=lax.Precision.HIGHEST)
    residual = kinetic + (local_potential[None] - band_energy[:, None, None]) * resp_f32
    residual = residual - EXCHANGE_FRACTION * exchange + perturb * ground_state.astype(jnp.float32)
    return (projector, residual)


def solution(mesh):
    return jax.shard_map(
        on_device,
        mesh=mesh,
        in_specs=(
            P(("grp", "band"), "ga", None),
            P("band", "ga", None),
            P("band", "ga", None),
            P("band"),
            P("band"),
            P("ga", None),
            P(None, "ga", None),
            P(None, "ga"),
        ),
        out_specs=(P("band", "ga", None), P("band", "ga", None)),
        check_vma=False,
    )
```

profile of v0, /device:TPU:1, one launch (start us, length us, event | category | flops | bytes accessed | tf_op | source)
XLA Modules:
  0.0 852.1 jit_solution(6318215926119918230)
XLA Ops:
  10.4 676.8 %while.15 = (s32[]{:T(128)}, bf16[4,24,192]{2,1,0:T(8,128)(2,1)S(1)}, f32[8,24,192]{2,1,0:T(8,128)S(1)}, bf16[8,24,192]{2,1,0:T(8,128)(2,1)}, f32[192,24]{0,1:T(...) while((s32[]{:T(128)}, ...), condition=%wide.region_2.3_spmd.clone.clone, body=%wide.region_0.2_spmd.clone.clone.sunk | while | flops 228390912 | bytes 10679251 | solution.py:87
  14.3 19.7 %all_to_all.89 = bf16[8,2,9216]{2,1,0:T(2,128)(2,1)S(1)} all-to-all(bf16[8,2,9216]{2,1,0:T(2,128)(2,1)S(1)} %reshape.67), channel_id=1, replica_groups=mesh['grp'=2,'band'=16,'ga'=8] {'ga'}, dimensions={0} | all-to-all | bytes 589824 | tf_op jit(solution)/shard_map/while/body/eval_jaxpr/all_to_all | solution.py:48
  34.5 2.5 copy.125
  42.5 3.4 all-to-all-start.1
  45.9 4.0 collective-permute-start
  49.9 5.8 all-to-all-done.1
  56.2 2.5 copy.127
  64.7 12.1 %all_to_all.89 = bf16[8,2,9216]{2,1,0:T(2,128)(2,1)S(1)} all-to-all(bf16[8,2,9216]{2,1,0:T(2,128)(2,1)S(1)} %reshape.67), channel_id=1, replica_groups=mesh['grp'=2,'band'=16,'ga'=8] {'ga'}, dimensions={0} | all-to-all | bytes 589824 | tf_op jit(solution)/shard_map/while/body/eval_jaxpr/all_to_all | solution.py:48
  77.3 2.5 copy.125
  85.3 3.4 all-to-all-start.1
  88.7 6.1 collective-permute-start
  94.9 3.6 all-to-all-done.1
  99.0 2.5 copy.127
  107.5 12.7 %all_to_all.89 = bf16[8,2,9216]{2,1,0:T(2,128)(2,1)S(1)} all-to-all(bf16[8,2,9216]{2,1,0:T(2,128)(2,1)S(1)} %reshape.67), channel_id=1, replica_groups=mesh['grp'=2,'band'=16,'ga'=8] {'ga'}, dimensions={0} | all-to-all | bytes 589824 | tf_op jit(solution)/shard_map/while/body/eval_jaxpr/all_to_all | solution.py:48
  128.7 3.4 all-to-all-start.1
  132.2 7.7 collective-permute-start
  150.8 14.3 %all_to_all.89 = bf16[8,2,9216]{2,1,0:T(2,128)(2,1)S(1)} all-to-all(bf16[8,2,9216]{2,1,0:T(2,128)(2,1)S(1)} %reshape.67), channel_id=1, replica_groups=mesh['grp'=2,'band'=16,'ga'=8] {'ga'}, dimensions={0} | all-to-all | bytes 589824 | tf_op jit(solution)/shard_map/while/body/eval_jaxpr/all_to_all | solution.py:48
  165.7 2.5 copy.125
  173.7 3.4 all-to-all-start.1
  177.1 7.7 collective-permute-start
  195.8 14.3 %all_to_all.89 = bf16[8,2,9216]{2,1,0:T(2,128)(2,1)S(1)} all-to-all(bf16[8,2,9216]{2,1,0:T(2,128)(2,1)S(1)} %reshape.67), channel_id=1, replica_groups=mesh['grp'=2,'band'=16,'ga'=8] {'ga'}, dimensions={0} | all-to-all | bytes 589824 | tf_op jit(solution)/shard_map/while/body/eval_jaxpr/all_to_all | solution.py:48
  210.7 2.5 copy.125
  218.7 3.4 all-to-all-start.1
  222.1 7.7 collective-permute-start
  240.8 14.3 %all_to_all.89 = bf16[8,2,9216]{2,1,0:T(2,128)(2,1)S(1)} all-to-all(bf16[8,2,9216]{2,1,0:T(2,128)(2,1)S(1)} %reshape.67), channel_id=1, replica_groups=mesh['grp'=2,'band'=16,'ga'=8] {'ga'}, dimensions={0} | all-to-all | bytes 589824 | tf_op jit(solution)/shard_map/while/body/eval_jaxpr/all_to_all | solution.py:48
  263.7 3.4 all-to-all-start.1
  267.1 7.7 collective-permute-start
  285.8 14.3 %all_to_all.89 = bf16[8,2,9216]{2,1,0:T(2,128)(2,1)S(1)} all-to-all(bf16[8,2,9216]{2,1,0:T(2,128)(2,1)S(1)} %reshape.67), channel_id=1, replica_groups=mesh['grp'=2,'band'=16,'ga'=8] {'ga'}, dimensions={0} | all-to-all | bytes 589824 | tf_op jit(solution)/shard_map/while/body/eval_jaxpr/all_to_all | solution.py:48
  308.6 3.4 all-to-all-start.1
  312.1 7.7 collective-permute-start
  330.8 14.3 %all_to_all.89 = bf16[8,2,9216]{2,1,0:T(2,128)(2,1)S(1)} all-to-all(bf16[8,2,9216]{2,1,0:T(2,128)(2,1)S(1)} %reshape.67), channel_id=1, replica_groups=mesh['grp'=2,'band'=16,'ga'=8] {'ga'}, dimensions={0} | all-to-all | bytes 589824 | tf_op jit(solution)/shard_map/while/body/eval_jaxpr/all_to_all | solution.py:48
  353.6 3.4 all-to-all-start.1
  357.1 7.7 collective-permute-start
  375.7 14.3 %all_to_all.89 = bf16[8,2,9216]{2,1,0:T(2,128)(2,1)S(1)} all-to-all(bf16[8,2,9216]{2,1,0:T(2,128)(2,1)S(1)} %reshape.67), channel_id=1, replica_groups=mesh['grp'=2,'band'=16,'ga'=8] {'ga'}, dimensions={0} | all-to-all | bytes 589824 | tf_op jit(solution)/shard_map/while/body/eval_jaxpr/all_to_all | solution.py:48
  398.6 3.4 all-to-all-start.1
  402.0 7.7 collective-permute-start
  420.7 14.3 %all_to_all.89 = bf16[8,2,9216]{2,1,0:T(2,128)(2,1)S(1)} all-to-all(bf16[8,2,9216]{2,1,0:T(2,128)(2,1)S(1)} %reshape.67), channel_id=1, replica_groups=mesh['grp'=2,'band'=16,'ga'=8] {'ga'}, dimensions={0} | all-to-all | bytes 589824 | tf_op jit(solution)/shard_map/while/body/eval_jaxpr/all_to_all | solution.py:48
  443.6 3.4 all-to-all-start.1
  447.0 7.7 collective-permute-start
  465.7 14.3 %all_to_all.89 = bf16[8,2,9216]{2,1,0:T(2,128)(2,1)S(1)} all-to-all(bf16[8,2,9216]{2,1,0:T(2,128)(2,1)S(1)} %reshape.67), channel_id=1, replica_groups=mesh['grp'=2,'band'=16,'ga'=8] {'ga'}, dimensions={0} | all-to-all | bytes 589824 | tf_op jit(solution)/shard_map/while/body/eval_jaxpr/all_to_all | solution.py:48
  488.6 3.4 all-to-all-start.1
  492.0 7.7 collective-permute-start
  510.7 14.3 %all_to_all.89 = bf16[8,2,9216]{2,1,0:T(2,128)(2,1)S(1)} all-to-all(bf16[8,2,9216]{2,1,0:T(2,128)(2,1)S(1)} %reshape.67), channel_id=1, replica_groups=mesh['grp'=2,'band'=16,'ga'=8] {'ga'}, dimensions={0} | all-to-all | bytes 589824 | tf_op jit(solution)/shard_map/while/body/eval_jaxpr/all_to_all | solution.py:48
  533.6 3.4 all-to-all-start.1
  537.0 7.7 collective-permute-start
  555.7 14.3 %all_to_all.89 = bf16[8,2,9216]{2,1,0:T(2,128)(2,1)S(1)} all-to-all(bf16[8,2,9216]{2,1,0:T(2,128)(2,1)S(1)} %reshape.67), channel_id=1, replica_groups=mesh['grp'=2,'band'=16,'ga'=8] {'ga'}, dimensions={0} | all-to-all | bytes 589824 | tf_op jit(solution)/shard_map/while/body/eval_jaxpr/all_to_all | solution.py:48
  578.5 3.4 all-to-all-start.1
  582.0 7.7 collective-permute-start
  600.6 14.3 %all_to_all.89 = bf16[8,2,9216]{2,1,0:T(2,128)(2,1)S(1)} all-to-all(bf16[8,2,9216]{2,1,0:T(2,128)(2,1)S(1)} %reshape.67), channel_id=1, replica_groups=mesh['grp'=2,'band'=16,'ga'=8] {'ga'}, dimensions={0} | all-to-all | bytes 589824 | tf_op jit(solution)/shard_map/while/body/eval_jaxpr/all_to_all | solution.py:48
  623.5 3.4 all-to-all-start.1
  626.9 7.7 collective-permute-start
  645.6 14.3 %all_to_all.89 = bf16[8,2,9216]{2,1,0:T(2,128)(2,1)S(1)} all-to-all(bf16[8,2,9216]{2,1,0:T(2,128)(2,1)S(1)} %reshape.67), channel_id=1, replica_groups=mesh['grp'=2,'band'=16,'ga'=8] {'ga'}, dimensions={0} | all-to-all | bytes 589824 | tf_op jit(solution)/shard_map/while/body/eval_jaxpr/all_to_all | solution.py:48
  668.5 3.4 all-to-all-start.1
  671.9 7.7 collective-permute-start
  690.2 14.3 %all_to_all.87 = bf16[8,2,9216]{2,1,0:T(2,128)(2,1)S(1)} all-to-all(bf16[8,2,9216]{2,1,0:T(2,128)(2,1)S(1)} %reshape.59), channel_id=1, replica_groups=mesh['grp'=2,'band'=16,'ga'=8] {'ga'}, dimensions={0} | all-to-all | bytes 589824 | tf_op jit(solution)/shard_map/all_to_all | solution.py:48
  705.1 2.5 copy.83
  712.4 12.2 %all_to_all.88 = bf16[8,2,9216]{2,1,0:T(2,128)(2,1)S(1)} all-to-all(bf16[8,2,9216]{2,1,0:T(2,128)(2,1)S(1)} %reshape.61), channel_id=1, replica_groups=mesh['grp'=2,'band'=16,'ga'=8] {'ga'}, dimensions={0} | all-to-all | bytes 589824 | tf_op jit(solution)/shard_map/all_to_all | solution.py:55
  731.2 38.8 %all-reduce.2.cloned.1.call-done = f32[8,24,192]{2,0,1:T(8,128)} async-done(((f32[8,24,192]{2,0,1:T(8,128)}), f32[8,24,192]{2,0,1:T(8,128)}) %all-reduce.2.cloned.1.call-update) | async-done | bytes 147472 | tf_op jit(solution)/shard_map/psum | solution.py:89
  771.7 3.1 collective-permute-start.1
  775.6 2.9 collective-permute-done.2
  781.5 10.7 %psum.15 = f32[128,8]{0,1:T(8,128)S(1)} all-reduce(f32[128,8]{0,1:T(8,128)S(1)} %fusion.41), channel_id=1, replica_groups=mesh['grp'=2,'band'=16,'ga'=8] {'ga'}, use_global_device_ids=true, to_apply=%region_5.6 | all-reduce | flops 1024 | bytes 8192 | tf_op jit(solution)/shard_map/psum | solution.py:103
  792.2 24.4 %all_gather.10 = f32[128,128]{0,1:T(8,128)S(1)} all-gather(f32[128,8]{0,1:T(8,128)S(1)} %psum.15), channel_id=1, replica_groups=mesh['grp'=2,'band'=16,'ga'=8] {'band'}, dimensions={1}, use_global_device_ids=true | all-gather | bytes 69632 | tf_op jit(solution)/shard_map/all_gather | solution.py:104
  816.9 11.7 %cholesky.17 = f32[128,128]{1,0:T(8,128)S(1)} custom-call(f32[128,128]{1,0:T(8,128)S(1)} %fusion.71), custom_call_target="Cholesky" | custom-call | tf_op jit(solution)/shard_map/jit(cholesky)/cholesky | solution.py:106
  829.9 9.8 %custom-call.6 = f32[1,128,128]{1,2,0:T(8,128)S(1)} custom-call(f32[1,128,128]{2,1,0:T(8,128)S(1)} %fusion.68), custom_call_target="InvertDiagBlocksLowerTriangular" | custom-call | tf_op jit(solution)/shard_map/triangular_solve | solution.py:107
  (389 shorter events, 300.6 us)
Async XLA Ops:
  8.0 770.5 %copy-start = (f32[3,24,192]{2,1,0:T(8,128)S(1)}, f32[3,24,192]{2,1,0:T(8,128)}, u32[]{:S(2)}) copy-start(f32[3,24,192]{2,1,0:T(8,128)} %param.16) | copy-start | bytes 165892
  8.0 762.0 %all-reduce.2.cloned.1.call-start = ((), (), s32[]{:S(2)}) async-start(), calls=%async_computation.4 | async-start | bytes 393216 | tf_op jit(solution)/shard_map/psum | solution.py:89
  37.0 1.1 copy-start.5
  42.5 13.2 %all-to-all-start.1 = ((bf16[8,2,9216]{2,1,0:T(2,128)(2,1)}), bf16[8,2,9216]{2,1,0:T(2,128)(2,1)S(1)}, u32[]{:S(2)}, u32[]{:S(2)}) async-start(bf16[8,2,9216]{2,1,0:T(2,128)(2,1)} %reshape.69), calls=%async_computation.1 | async-start | bytes 589824 | tf_op jit(solution)/shard_map/while/body/eval_jaxpr/all_to_all | solution.py:55
  45.9 14.9 %collective-permute-start = (bf16[4,24,192]{2,1,0:T(8,128)(2,1)S(1)}, bf16[4,24,192]{2,1,0:T(8,128)(2,1)S(1)}, u32[]{:S(2)}, u32[]{:S(2)}) collective-permute-start(bf16[4,24,192]{2,1,0:T(8,128)(2,1)S(1)} %copy.132), channel_id=1, source_target_pairs={{0,8},{8,16},{16,24},{24,32},{32,40},{40,48},{48,56},{56,64},{64,7... | collective-permute-start | bytes 110600 | tf_op jit(solution)/shard_map/while/body/eval_jaxpr/ppermute | solution.py:11
  79.8 1.1 copy-start.5
  85.3 13.1 %all-to-all-start.1 = ((bf16[8,2,9216]{2,1,0:T(2,128)(2,1)}), bf16[8,2,9216]{2,1,0:T(2,128)(2,1)S(1)}, u32[]{:S(2)}, u32[]{:S(2)}) async-start(bf16[8,2,9216]{2,1,0:T(2,128)(2,1)} %reshape.69), calls=%async_computation.1 | async-start | bytes 589824 | tf_op jit(solution)/shard_map/while/body/eval_jaxpr/all_to_all | solution.py:55
  88.7 14.9 %collective-permute-start = (bf16[4,24,192]{2,1,0:T(8,128)(2,1)S(1)}, bf16[4,24,192]{2,1,0:T(8,128)(2,1)S(1)}, u32[]{:S(2)}, u32[]{:S(2)}) collective-permute-start(bf16[4,24,192]{2,1,0:T(8,128)(2,1)S(1)} %copy.132), channel_id=1, source_target_pairs={{0,8},{8,16},{16,24},{24,32},{32,40},{40,48},{48,56},{56,64},{64,7... | collective-permute-start | bytes 110600 | tf_op jit(solution)/shard_map/while/body/eval_jaxpr/ppermute | solution.py:11
  123.3 1.1 copy-start.5
  128.7 13.0 %all-to-all-start.1 = ((bf16[8,2,9216]{2,1,0:T(2,128)(2,1)}), bf16[8,2,9216]{2,1,0:T(2,128)(2,1)S(1)}, u32[]{:S(2)}, u32[]{:S(2)}) async-start(bf16[8,2,9216]{2,1,0:T(2,128)(2,1)} %reshape.69), calls=%async_computation.1 | async-start | bytes 589824 | tf_op jit(solution)/shard_map/while/body/eval_jaxpr/all_to_all | solution.py:55
  132.2 14.8 %collective-permute-start = (bf16[4,24,192]{2,1,0:T(8,128)(2,1)S(1)}, bf16[4,24,192]{2,1,0:T(8,128)(2,1)S(1)}, u32[]{:S(2)}, u32[]{:S(2)}) collective-permute-start(bf16[4,24,192]{2,1,0:T(8,128)(2,1)S(1)} %copy.132), channel_id=1, source_target_pairs={{0,8},{8,16},{16,24},{24,32},{32,40},{40,48},{48,56},{56,64},{64,7... | collective-permute-start | bytes 110600 | tf_op jit(solution)/shard_map/while/body/eval_jaxpr/ppermute | solution.py:11
  168.3 1.1 copy-start.5
  173.7 13.0 %all-to-all-start.1 = ((bf16[8,2,9216]{2,1,0:T(2,128)(2,1)}), bf16[8,2,9216]{2,1,0:T(2,128)(2,1)S(1)}, u32[]{:S(2)}, u32[]{:S(2)}) async-start(bf16[8,2,9216]{2,1,0:T(2,128)(2,1)} %reshape.69), calls=%async_computation.1 | async-start | bytes 589824 | tf_op jit(solution)/shard_map/while/body/eval_jaxpr/all_to_all | solution.py:55
  177.1 14.8 %collective-permute-start = (bf16[4,24,192]{2,1,0:T(8,128)(2,1)S(1)}, bf16[4,24,192]{2,1,0:T(8,128)(2,1)S(1)}, u32[]{:S(2)}, u32[]{:S(2)}) collective-permute-start(bf16[4,24,192]{2,1,0:T(8,128)(2,1)S(1)} %copy.132), channel_id=1, source_target_pairs={{0,8},{8,16},{16,24},{24,32},{32,40},{40,48},{48,56},{56,64},{64,7... | collective-permute-start | bytes 110600 | tf_op jit(solution)/shard_map/while/body/eval_jaxpr/ppermute | solution.py:11
  213.2 1.1 copy-start.5
  218.7 13.0 %all-to-all-start.1 = ((bf16[8,2,9216]{2,1,0:T(2,128)(2,1)}), bf16[8,2,9216]{2,1,0:T(2,128)(2,1)S(1)}, u32[]{:S(2)}, u32[]{:S(2)}) async-start(bf16[8,2,9216]{2,1,0:T(2,128)(2,1)} %reshape.69), calls=%async_computation.1 | async-start | bytes 589824 | tf_op jit(solution)/shard_map/while/body/eval_jaxpr/all_to_all | solution.py:55
  222.1 14.8 %collective-permute-start = (bf16[4,24,192]{2,1,0:T(8,128)(2,1)S(1)}, bf16[4,24,192]{2,1,0:T(8,128)(2,1)S(1)}, u32[]{:S(2)}, u32[]{:S(2)}) collective-permute-start(bf16[4,24,192]{2,1,0:T(8,128)(2,1)S(1)} %copy.132), channel_id=1, source_target_pairs={{0,8},{8,16},{16,24},{24,32},{32,40},{40,48},{48,56},{56,64},{64,7... | collective-permute-start | bytes 110600 | tf_op jit(solution)/shard_map/while/body/eval_jaxpr/ppermute | solution.py:11
  258.2 1.1 copy-start.5
  263.7 13.0 %all-to-all-start.1 = ((bf16[8,2,9216]{2,1,0:T(2,128)(2,1)}), bf16[8,2,9216]{2,1,0:T(2,128)(2,1)S(1)}, u32[]{:S(2)}, u32[]{:S(2)}) async-start(bf16[8,2,9216]{2,1,0:T(2,128)(2,1)} %reshape.69), calls=%async_computation.1 | async-start | bytes 589824 | tf_op jit(solution)/shard_map/while/body/eval_jaxpr/all_to_all | solution.py:55
  267.1 14.8 %collective-permute-start = (bf16[4,24,192]{2,1,0:T(8,128)(2,1)S(1)}, bf16[4,24,192]{2,1,0:T(8,128)(2,1)S(1)}, u32[]{:S(2)}, u32[]{:S(2)}) collective-permute-start(bf16[4,24,192]{2,1,0:T(8,128)(2,1)S(1)} %copy.132), channel_id=1, source_target_pairs={{0,8},{8,16},{16,24},{24,32},{32,40},{40,48},{48,56},{56,64},{64,7... | collective-permute-start | bytes 110600 | tf_op jit(solution)/shard_map/while/body/eval_jaxpr/ppermute | solution.py:11
  303.2 1.1 copy-start.5
  308.6 13.0 %all-to-all-start.1 = ((bf16[8,2,9216]{2,1,0:T(2,128)(2,1)}), bf16[8,2,9216]{2,1,0:T(2,128)(2,1)S(1)}, u32[]{:S(2)}, u32[]{:S(2)}) async-start(bf16[8,2,9216]{2,1,0:T(2,128)(2,1)} %reshape.69), calls=%async_computation.1 | async-start | bytes 589824 | tf_op jit(solution)/shard_map/while/body/eval_jaxpr/all_to_all | solution.py:55
  312.1 14.8 %collective-permute-start = (bf16[4,24,192]{2,1,0:T(8,128)(2,1)S(1)}, bf16[4,24,192]{2,1,0:T(8,128)(2,1)S(1)}, u32[]{:S(2)}, u32[]{:S(2)}) collective-permute-start(bf16[4,24,192]{2,1,0:T(8,128)(2,1)S(1)} %copy.132), channel_id=1, source_target_pairs={{0,8},{8,16},{16,24},{24,32},{32,40},{40,48},{48,56},{56,64},{64,7... | collective-permute-start | bytes 110600 | tf_op jit(solution)/shard_map/while/body/eval_jaxpr/ppermute | solution.py:11
  348.2 1.1 copy-start.5
  353.6 13.0 %all-to-all-start.1 = ((bf16[8,2,9216]{2,1,0:T(2,128)(2,1)}), bf16[8,2,9216]{2,1,0:T(2,128)(2,1)S(1)}, u32[]{:S(2)}, u32[]{:S(2)}) async-start(bf16[8,2,9216]{2,1,0:T(2,128)(2,1)} %reshape.69), calls=%async_computation.1 | async-start | bytes 589824 | tf_op jit(solution)/shard_map/while/body/eval_jaxpr/all_to_all | solution.py:55
  357.1 14.8 %collective-permute-start = (bf16[4,24,192]{2,1,0:T(8,128)(2,1)S(1)}, bf16[4,24,192]{2,1,0:T(8,128)(2,1)S(1)}, u32[]{:S(2)}, u32[]{:S(2)}) collective-permute-start(bf16[4,24,192]{2,1,0:T(8,128)(2,1)S(1)} %copy.132), channel_id=1, source_target_pairs={{0,8},{8,16},{16,24},{24,32},{32,40},{40,48},{48,56},{56,64},{64,7... | collective-permute-start | bytes 110600 | tf_op jit(solution)/shard_map/while/body/eval_jaxpr/ppermute | solution.py:11
  393.2 1.1 copy-start.5
  398.6 13.0 %all-to-all-start.1 = ((bf16[8,2,9216]{2,1,0:T(2,128)(2,1)}), bf16[8,2,9216]{2,1,0:T(2,128)(2,1)S(1)}, u32[]{:S(2)}, u32[]{:S(2)}) async-start(bf16[8,2,9216]{2,1,0:T(2,128)(2,1)} %reshape.69), calls=%async_computation.1 | async-start | bytes 589824 | tf_op jit(solution)/shard_map/while/body/eval_jaxpr/all_to_all | solution.py:55
  402.0 14.8 %collective-permute-start = (bf16[4,24,192]{2,1,0:T(8,128)(2,1)S(1)}, bf16[4,24,192]{2,1,0:T(8,128)(2,1)S(1)}, u32[]{:S(2)}, u32[]{:S(2)}) collective-permute-start(bf16[4,24,192]{2,1,0:T(8,128)(2,1)S(1)} %copy.132), channel_id=1, source_target_pairs={{0,8},{8,16},{16,24},{24,32},{32,40},{40,48},{48,56},{56,64},{64,7... | collective-permute-start | bytes 110600 | tf_op jit(solution)/shard_map/while/body/eval_jaxpr/ppermute | solution.py:11
  438.1 1.1 copy-start.5
  443.6 13.0 %all-to-all-start.1 = ((bf16[8,2,9216]{2,1,0:T(2,128)(2,1)}), bf16[8,2,9216]{2,1,0:T(2,128)(2,1)S(1)}, u32[]{:S(2)}, u32[]{:S(2)}) async-start(bf16[8,2,9216]{2,1,0:T(2,128)(2,1)} %reshape.69), calls=%async_computation.1 | async-start | bytes 589824 | tf_op jit(solution)/shard_map/while/body/eval_jaxpr/all_to_all | solution.py:55
  447.0 14.8 %collective-permute-start = (bf16[4,24,192]{2,1,0:T(8,128)(2,1)S(1)}, bf16[4,24,192]{2,1,0:T(8,128)(2,1)S(1)}, u32[]{:S(2)}, u32[]{:S(2)}) collective-permute-start(bf16[4,24,192]{2,1,0:T(8,128)(2,1)S(1)} %copy.132), channel_id=1, source_target_pairs={{0,8},{8,16},{16,24},{24,32},{32,40},{40,48},{48,56},{56,64},{64,7... | collective-permute-start | bytes 110600 | tf_op jit(solution)/shard_map/while/body/eval_jaxpr/ppermute | solution.py:11
  483.1 1.1 copy-start.5
  488.6 13.0 %all-to-all-start.1 = ((bf16[8,2,9216]{2,1,0:T(2,128)(2,1)}), bf16[8,2,9216]{2,1,0:T(2,128)(2,1)S(1)}, u32[]{:S(2)}, u32[]{:S(2)}) async-start(bf16[8,2,9216]{2,1,0:T(2,128)(2,1)} %reshape.69), calls=%async_computation.1 | async-start | bytes 589824 | tf_op jit(solution)/shard_map/while/body/eval_jaxpr/all_to_all | solution.py:55
  492.0 14.8 %collective-permute-start = (bf16[4,24,192]{2,1,0:T(8,128)(2,1)S(1)}, bf16[4,24,192]{2,1,0:T(8,128)(2,1)S(1)}, u32[]{:S(2)}, u32[]{:S(2)}) collective-permute-start(bf16[4,24,192]{2,1,0:T(8,128)(2,1)S(1)} %copy.132), channel_id=1, source_target_pairs={{0,8},{8,16},{16,24},{24,32},{32,40},{40,48},{48,56},{56,64},{64,7... | collective-permute-start | bytes 110600 | tf_op jit(solution)/shard_map/while/body/eval_jaxpr/ppermute | solution.py:11
  528.1 1.1 copy-start.5
  533.6 13.0 %all-to-all-start.1 = ((bf16[8,2,9216]{2,1,0:T(2,128)(2,1)}), bf16[8,2,9216]{2,1,0:T(2,128)(2,1)S(1)}, u32[]{:S(2)}, u32[]{:S(2)}) async-start(bf16[8,2,9216]{2,1,0:T(2,128)(2,1)} %reshape.69), calls=%async_computation.1 | async-start | bytes 589824 | tf_op jit(solution)/shard_map/while/body/eval_jaxpr/all_to_all | solution.py:55
  537.0 14.8 %collective-permute-start = (bf16[4,24,192]{2,1,0:T(8,128)(2,1)S(1)}, bf16[4,24,192]{2,1,0:T(8,128)(2,1)S(1)}, u32[]{:S(2)}, u32[]{:S(2)}) collective-permute-start(bf16[4,24,192]{2,1,0:T(8,128)(2,1)S(1)} %copy.132), channel_id=1, source_target_pairs={{0,8},{8,16},{16,24},{24,32},{32,40},{40,48},{48,56},{56,64},{64,7... | collective-permute-start | bytes 110600 | tf_op jit(solution)/shard_map/while/body/eval_jaxpr/ppermute | solution.py:11
  573.1 1.1 copy-start.5
  578.5 13.0 %all-to-all-start.1 = ((bf16[8,2,9216]{2,1,0:T(2,128)(2,1)}), bf16[8,2,9216]{2,1,0:T(2,128)(2,1)S(1)}, u32[]{:S(2)}, u32[]{:S(2)}) async-start(bf16[8,2,9216]{2,1,0:T(2,128)(2,1)} %reshape.69), calls=%async_computation.1 | async-start | bytes 589824 | tf_op jit(solution)/shard_map/while/body/eval_jaxpr/all_to_all | solution.py:55
  582.0 14.8 %collective-permute-start = (bf16[4,24,192]{2,1,0:T(8,128)(2,1)S(1)}, bf16[4,24,192]{2,1,0:T(8,128)(2,1)S(1)}, u32[]{:S(2)}, u32[]{:S(2)}) collective-permute-start(bf16[4,24,192]{2,1,0:T(8,128)(2,1)S(1)} %copy.132), channel_id=1, source_target_pairs={{0,8},{8,16},{16,24},{24,32},{32,40},{40,48},{48,56},{56,64},{64,7... | collective-permute-start | bytes 110600 | tf_op jit(solution)/shard_map/while/body/eval_jaxpr/ppermute | solution.py:11
  618.1 1.1 copy-start.5
  623.5 13.0 %all-to-all-start.1 = ((bf16[8,2,9216]{2,1,0:T(2,128)(2,1)}), bf16[8,2,9216]{2,1,0:T(2,128)(2,1)S(1)}, u32[]{:S(2)}, u32[]{:S(2)}) async-start(bf16[8,2,9216]{2,1,0:T(2,128)(2,1)} %reshape.69), calls=%async_computation.1 | async-start | bytes 589824 | tf_op jit(solution)/shard_map/while/body/eval_jaxpr/all_to_all | solution.py:55
  626.9 14.8 %collective-permute-start = (bf16[4,24,192]{2,1,0:T(8,128)(2,1)S(1)}, bf16[4,24,192]{2,1,0:T(8,128)(2,1)S(1)}, u32[]{:S(2)}, u32[]{:S(2)}) collective-permute-start(bf16[4,24,192]{2,1,0:T(8,128)(2,1)S(1)} %copy.132), channel_id=1, source_target_pairs={{0,8},{8,16},{16,24},{24,32},{32,40},{40,48},{48,56},{56,64},{64,7... | collective-permute-start | bytes 110600 | tf_op jit(solution)/shard_map/while/body/eval_jaxpr/ppermute | solution.py:11
  663.0 1.1 copy-start.5
  668.5 13.0 %all-to-all-start.1 = ((bf16[8,2,9216]{2,1,0:T(2,128)(2,1)}), bf16[8,2,9216]{2,1,0:T(2,128)(2,1)S(1)}, u32[]{:S(2)}, u32[]{:S(2)}) async-start(bf16[8,2,9216]{2,1,0:T(2,128)(2,1)} %reshape.69), calls=%async_computation.1 | async-start | bytes 589824 | tf_op jit(solution)/shard_map/while/body/eval_jaxpr/all_to_all | solution.py:55
  671.9 14.8 %collective-permute-start = (bf16[4,24,192]{2,1,0:T(8,128)(2,1)S(1)}, bf16[4,24,192]{2,1,0:T(8,128)(2,1)S(1)}, u32[]{:S(2)}, u32[]{:S(2)}) collective-permute-start(bf16[4,24,192]{2,1,0:T(8,128)(2,1)S(1)} %copy.132), channel_id=1, source_target_pairs={{0,8},{8,16},{16,24},{24,32},{32,40},{40,48},{48,56},{56,64},{64,7... | collective-permute-start | bytes 110600 | tf_op jit(solution)/shard_map/while/body/eval_jaxpr/ppermute | solution.py:11
  707.6 1.1 copy-start.6
  728.7 43.0 %copy-start.2 = (bf16[8,24,192]{2,0,1:T(8,128)(2,1)S(1)}, bf16[8,24,192]{2,0,1:T(8,128)(2,1)}, u32[]{:S(2)}) copy-start(bf16[8,24,192]{2,0,1:T(8,128)(2,1)} %get-tuple-element.144) | copy-start | bytes 221188
  729.7 48.8 %copy-start.4 = (bf16[8,24,192]{2,1,0:T(8,128)(2,1)S(1)}, bf16[8,24,192]{2,1,0:T(8,128)(2,1)}, u32[]{:S(2)}) copy-start(bf16[8,24,192]{2,1,0:T(8,128)(2,1)} %param.12) | copy-start | bytes 221188
  729.7 48.7 %copy-start.7 = (f32[24,192]{1,0:T(8,128)S(1)}, f32[24,192]{1,0:T(8,128)}, u32[]{:S(2)}) copy-start(f32[24,192]{1,0:T(8,128)} %param.15) | copy-start | bytes 55300
  729.8 48.7 %copy-start.8 = (f32[8]{0:T(128)S(1)}, f32[8]{0:T(128)}, u32[]{:S(2)}) copy-start(f32[8]{0:T(128)} %param.14) | copy-start | bytes 100
  729.8 48.7 %copy-start.9 = (s32[8]{0:T(128)S(1)}, s32[8]{0:T(128)}, u32[]{:S(2)}) copy-start(s32[8]{0:T(128)} %param.13) | copy-start | bytes 100
  730.6 49.0 %all-gather.3.cloned.1.call-start = ((), (), s32[]{:S(2)}) async-start(), calls=%async_computation.5 | async-start | bytes 1671168 | tf_op jit(solution)/shard_map/all_gather | solution.py:96
  731.2 108.8 %all-gather.5.cloned.1.call-start = ((), (), s32[]{:S(2)}) async-start(), calls=%async_computation.6 | async-start | bytes 1671168 | tf_op jit(solution)/shard_map/all_gather | solution.py:111
  770.0 8.5 copy-start.3
  771.7 3.9 collective-permute-start.1
  774.8 3.7 collective-permute-start.2
  774.9 4.7 copy-start.1
Sparse Core Ops, SparseCore 0:
  730.7 39.2 all-reduce.1
Sparse Core Ops, SparseCore 1:
  733.4 42.0 all-gather.2
  777.1 38.4 all-gather.4
where the time goes:
time: 865 us; the launch traced here: 852 us
  blocking collectives  278 us (32%)
  local copies, waits for them, and re-layouts  206 us (24%)
  starting transfers between devices  165 us (19%)
  waiting for transfers between devices  77 us (9%)
  matrix products  65 us (8%)
  other arithmetic  42.7 us (5%)
  between operations  16 us (2%)
    all_to_all x16, blocking collectives, pair_field(): lax.all_to_all(first, 'ga', split_axis=2, concat_axis=1, tiled=True)  231 us
    ppermute x15, starting transfers between devices, passed_along(): lax.ppermute(x, axis, [(i, (i + by) % devices) for i in range(devices)])  110 us
    while x105, local copies, waits for them, and re-layouts  60.9 us
    all_to_all x32, local copies, waits for them, and re-layouts, pair_field(): lax.all_to_all(first, 'ga', split_axis=2, concat_axis=1, tiled=True)  56.8 us
    all_to_all x15, starting transfers between devices, pair_field(): lax.all_to_all(third, 'ga', split_axis=1, concat_axis=2, tiled=True)  51.3 us
    all_to_all x16, local copies, waits for them, and re-layouts, pair_field(): lax.all_to_all(third, 'ga', split_axis=1, concat_axis=2, tiled=True)  40.3 us
    psum x1, waiting for transfers between devices, on_device(): exchange = lax.psum(total, 'grp')  38.8 us
    all_to_all x15, waiting for transfers between devices, pair_field(): lax.all_to_all(third, 'ga', split_axis=1, concat_axis=2, tiled=True)  34.2 us
  transfers between devices with their start and end apart: 35, of which 18 were waited for; matrix products, arithmetic and copies ran while one was open for 12% of the time, Pallas kernels for 0%

commit v1 on v0

v1 whole, which is shorter than its diff:
```python
import functools

import jax
import jax.numpy as jnp
import ml_dtypes
import numpy as np
from jax import lax
from jax.experimental import pallas as pl
from jax.experimental.pallas import tpu as pltpu
from jax.sharding import PartitionSpec as P

EXCHANGE_FRACTION = 0.25
F32, BF16 = jnp.float32, jnp.bfloat16
MESH = pl.DeviceIdType.MESH
N = 192
NZ = 8
SLAB = N // NZ
HALF = N // 2
BANDS = 128


def cosine_table(length):
    rows = np.arange(length, dtype=np.float32)[:, None]
    cols = np.arange(length, dtype=np.float32)[None]
    one, two = np.sqrt(np.float32(1.0 / length)), np.sqrt(np.float32(2.0 / length))
    factor = np.where(rows == 0, one, two).astype(np.float32)
    angle = np.float32(np.pi) * (cols + np.float32(0.5)) * rows / np.float32(length)
    return (factor * np.cos(angle)).astype(ml_dtypes.bfloat16)


def inverse_factor(gram):
    lane = lax.broadcasted_iota(jnp.int32, (8, BANDS), 1)
    sub = lax.broadcasted_iota(jnp.int32, (8, BANDS), 0)
    count = BANDS // 8
    blocks = [gram[8 * i : 8 * i + 8, :] for i in range(count)]
    done = []
    for b in range(count):
        k0 = 8 * b
        inside = (lane >= k0) & (lane < k0 + 8)
        rows = [jnp.broadcast_to(blocks[b][t : t + 1, :], (8, BANDS)) for t in range(8)]
        a = [
            [jnp.broadcast_to(rows[t][:, k0 + s : k0 + s + 1], (8, BANDS)) for s in range(t + 1)]
            for t in range(8)
        ]
        low = [[None] * 8 for _ in range(8)]
        rinv = [None] * 8
        for t in range(8):
            rinv[t] = lax.rsqrt(a[t][t])
            for u in range(t + 1, 8):
                low[u][t] = a[u][t] * rinv[t]
            for u in range(t + 1, 8):
                for s in range(t + 1, u + 1):
                    a[u][s] = a[u][s] - low[u][t] * low[s][t]
        inv = [[None] * 8 for _ in range(8)]
        for s in range(8):
            inv[s][s] = rinv[s]
            for t in range(s + 1, 8):
                acc = low[t][s] * inv[s][s]
                for u in range(s + 1, t):
                    acc = acc + low[t][u] * inv[u][s]
                inv[t][s] = -(acc * rinv[t])
        unit = [
            jnp.where(lane == k0 + t, 1.0, jnp.where(inside, 0.0, rows[t])) for t in range(8)
        ]
        panel = []
        for t in range(8):
            acc = inv[t][0] * unit[0]
            for s in range(1, t + 1):
                acc = acc + inv[t][s] * unit[s]
            panel.append(acc)
        packed = panel[0]
        for t in range(1, 8):
            packed = jnp.where(sub == t, panel[t], packed)
        done.append(jnp.where(lane <= sub + k0, packed, 0.0))
        for i in range(b + 1, count):
            column = [
                jnp.broadcast_to(blocks[i][:, k0 + s : k0 + s + 1], (8, BANDS)) for s in range(8)
            ]
            new = jnp.where(inside, 0.0, blocks[i])
            for t in range(8):
                factor = inv[t][0] * column[0]
                for s in range(1, t + 1):
                    factor = factor + inv[t][s] * column[s]
                new = new - factor * panel[t]
            blocks[i] = new
    return jnp.concatenate(done, axis=0)


def split_bf16(value):
    first = value.astype(BF16)
    rest = value - first.astype(F32)
    second = rest.astype(BF16)
    third = (rest - second.astype(F32)).astype(BF16)
    return [first.astype(F32), second.astype(F32), third.astype(F32)]


def mod4(i):
    return lax.rem(i, 4)


class PlaneGather:
    def __init__(self, place, ref, first, second, sib, got, got_sib):
        self.place, self.ref = place, ref
        self.s_first, self.s_second, self.s_sib = first, second, sib
        self.r_ici, self.r_sib = got, got_sib

    def slot(self, d, e):
        p = self.place
        f, s = mod4(p.f + d), mod4(p.s + e)
        return (1 - p.c) * (4 * s + f) + p.c * (4 * f + s)

    def peer(self, d, e):
        p = self.place
        f, s = mod4(p.f + d), mod4(p.s + e)
        return p.dev((1 - p.c) * f + p.c * s, (1 - p.c) * s + p.c * f, p.z, p.c)

    def copy(self, sl, half, send, recv, device):
        part = self.ref.at[sl, half]
        return pltpu.make_async_remote_copy(
            src_ref=part,
            dst_ref=part,
            send_sem=send,
            recv_sem=recv,
            device_id=device,
            device_id_type=MESH,
        )

    def first_copy(self, d):
        sl = self.slot(0, 0)
        return self.copy(sl, self.place.c, self.s_first.at[d - 1], self.r_ici.at[sl], self.peer(d, 0))

    def second_copy(self, d, e):
        sl = self.slot(d, 0)
        return self.copy(
            sl, self.place.c, self.s_second.at[3 * d + e - 1], self.r_ici.at[sl], self.peer(0, e)
        )

    def sib_copy(self, d, e):
        p = self.place
        sl = self.slot(d, e)
        return self.copy(sl, p.c, self.s_sib.at[4 * d + e], self.r_sib.at[sl], p.sibling)

    def start(self):
        for d in (1, 3, 2):
            self.first_copy(d).start()
        for e in (1, 3, 2):
            self.second_copy(0, e).start()
        self.sib_copy(0, 0).start()

    def forward(self):
        for d in (1, 3, 2):
            sl = self.slot(d, 0)
            self.copy(
                sl, self.place.c, self.s_first.at[0], self.r_ici.at[sl], self.peer(d, 0)
            ).wait_recv()
            for e in (1, 3, 2):
                self.second_copy(d, e).start()
            self.sib_copy(d, 0).start()

    def hand_on(self, e):
        for d in (0, 1, 3, 2):
            sl = self.slot(d, e)
            self.copy(
                sl, self.place.c, self.s_first.at[0], self.r_ici.at[sl], self.peer(0, e)
            ).wait_recv()
            self.sib_copy(d, e).start()

    def wait_sib(self, sl):
        p = self.place
        self.copy(sl, 1 - p.c, self.s_sib.at[0], self.r_sib.at[sl], p.sibling).wait_recv()

    def finish(self):
        for d in (1, 2, 3):
            self.first_copy(d).wait_send()
        for d in range(4):
            for e in (1, 2, 3):
                self.second_copy(d, e).wait_send()
        for d in range(4):
            for e in range(4):
                self.sib_copy(d, e).wait_send()


class Place:
    def __init__(self):
        self.g = lax.axis_index("grp")
        self.b = lax.axis_index("band")
        self.z = lax.axis_index("ga")
        self.x = lax.div(self.b, 4)
        self.y_lo = lax.rem(lax.div(self.b, 2), 2)
        self.c = lax.rem(self.b, 2)
        self.y = 2 * self.g + self.y_lo
        self.f = (1 - self.c) * self.x + self.c * self.y
        self.s = (1 - self.c) * self.y + self.c * self.x
        self.sibling = self.dev(self.x, self.y, self.z, 1 - self.c)

    def dev(self, x, y, z, c):
        return {"grp": lax.div(y, 2), "band": 4 * x + 2 * lax.rem(y, 2) + c, "ga": z}

    def z_peer(self, d, c):
        return self.dev(self.x, self.y, lax.rem(self.z + d, NZ), c)


def remote(src, dst, send, recv, device):
    return pltpu.make_async_remote_copy(
        src_ref=src,
        dst_ref=dst,
        send_sem=send,
        recv_sem=recv,
        device_id=device,
        device_id_type=MESH,
    )


Z_ORDER = (1, 7, 2, 6, 3, 5, 4)


def kernel(
    occ_ref,
    resp_ref,
    ground_ref,
    index_ref,
    energy_ref,
    local_ref,
    field_ref,
    table_ref,
    c_ref,
    ct_ref,
    proj_ref,
    res_ref,
    occ_src,
    occ_got,
    resp_got,
    resp_sib,
    resp_full,
    table_got,
    table,
    halo_src,
    halo_got,
    occ_all,
    resp_all,
    exch_all,
    total,
    rs_src,
    rs_got,
    rows32,
    exch_own,
    exch_wire,
    gram_z,
    gram_xy,
    gram_full,
    spread,
    proj32,
    *sems,
):
    p = Place()
    z, c, x, y, g = p.z, p.c, p.x, p.y, p.g
    sems = list(sems)
    take = lambda: sems.pop(0)
    occ_s, occ_r = take(), take()
    resp_s, resp_r = take(), take()
    sib_s, sib_r = take(), take()
    table_s, table_r = take(), take()
    halo_s, halo_r = take(), take()
    rs_s, rs_r = take(), take()
    gz_s, gz_r = take(), take()
    gx_s, gx_r = take(), take()
    gy_s, gy_r = take(), take()
    occ_gather = PlaneGather(p, occ_all, *[take() for _ in range(5)])
    resp_gather = PlaneGather(p, resp_all, *[take() for _ in range(5)])
    exch_gather = PlaneGather(p, exch_all, *[take() for _ in range(5)])

    barrier = pltpu.get_barrier_semaphore()
    peers = [p.z_peer(d, k) for d in range(1, NZ) for k in (0, 1)]
    peers += [p.sibling]
    peers += [p.dev(mod4(x + d), y, z, c) for d in (1, 2, 3)]
    peers += [p.dev(x, mod4(y + d), z, c) for d in (1, 2, 3)]
    for peer in peers:
        pl.semaphore_signal(barrier, inc=1, device_id=peer, device_id_type=MESH)

    table_got[z] = table_ref[...].T
    for r in range(4):
        occ_src[r] = occ_ref[r].astype(F32)
    for h in range(2):
        pair = [resp_ref[4 * g + 2 * h + r].astype(F32) for r in range(2)]
        resp_got[h, z] = jnp.concatenate(pair, axis=0).astype(BF16)
    edge = [resp_ref[j].astype(F32) for j in range(8)]
    halo_src[0] = jnp.concatenate([e[SLAB - 1 : SLAB] for e in edge], axis=0)
    halo_src[1] = jnp.concatenate([e[0:1] for e in edge], axis=0)
    pl.semaphore_wait(barrier, len(peers))

    half_of_z = lax.div(z, 4)
    quarter = lax.rem(z, 4)

    def occ_out(r):
        return remote(
            occ_src.at[r],
            occ_got.at[quarter],
            occ_s.at[r],
            occ_r.at[quarter],
            p.dev(x, y, 4 * c + r, half_of_z),
        )

    def occ_in(q):
        return remote(
            occ_src.at[q],
            occ_got.at[q],
            occ_s.at[q],
            occ_r.at[q],
            p.dev(x, y, 4 * c + q, half_of_z),
        )

    def mine(r):
        return (half_of_z == c) & (quarter == r)

    for r in range(4):
        @pl.when(jnp.logical_not(mine(r)))
        def _():
            occ_out(r).start()

        @pl.when(mine(r))
        def _():
            occ_got[r] = occ_src[r]

    def table_copy(d):
        return remote(table_got.at[z], table_got.at[z], table_s.at[d - 1], table_r.at[z], p.z_peer(d, c))

    def resp_copy(h, d):
        return remote(
            resp_got.at[h, z],
            resp_got.at[h, z],
            resp_s.at[7 * h + d - 1],
            resp_r.at[8 * h + z],
            p.z_peer(d, c),
        )

    def resp_wait(h, d):
        src = lax.rem(z + d, NZ)
        remote(
            resp_got.at[h, src],
            resp_got.at[h, src],
            resp_s.at[0],
            resp_r.at[8 * h + src],
            p.z_peer(d, c),
        ).wait_recv()

    def sib_resp(h):
        return remote(resp_got.at[h, z], resp_sib.at[h], sib_s.at[h], sib_r.at[h], p.sibling)

    def halo_copy(k):
        return remote(
            halo_src.at[k], halo_got.at[k], halo_s.at[k], halo_r.at[k], p.z_peer((1, 7)[k], c)
        )

    for d in Z_ORDER:
        resp_copy(0, d).start()
    for d in Z_ORDER:
        table_copy(d).start()
    for d in Z_ORDER:
        resp_copy(1, d).start()
    for h in range(2):
        sib_resp(h).start()
    for k in range(2):
        halo_copy(k).start()

    for q in range(4):
        @pl.when(jnp.logical_not(mine(q)))
        def _():
            occ_in(q).wait_recv()

    own = 4 * y + x
    occ_all[own, c] = jnp.concatenate([occ_got[q] for q in range(4)], axis=0).astype(BF16)
    occ_gather.start()

    def arrange(parts):
        for k in range(8):
            rows32[:, k, :] = parts[k]

    def by_core(mine_part, other_part):
        first = [jnp.where(c == 0, mine_part(r), other_part(r)) for r in range(4)]
        last = [jnp.where(c == 0, other_part(r), mine_part(r)) for r in range(4)]
        return first + last

    def rows_half():
        return rows32[pl.ds((SLAB // 2) * c, SLAB // 2)].reshape(HALF, N).astype(BF16)

    def slab_of(ref):
        def part(r):
            return ref(r // 2).astype(F32)[SLAB * (r % 2) : SLAB * (r % 2) + SLAB]

        return part

    for h in range(2):
        sib_resp(h).wait_recv()
    arrange(by_core(slab_of(lambda h: resp_got[h, z]), slab_of(lambda h: resp_sib[h])))
    resp_all[own, c] = rows_half()

    occ_gather.forward()

    def unpack(h):
        for d in Z_ORDER:
            resp_wait(h, d)
        for r in range(2):
            whole = [
                resp_got[h, s].astype(F32)[SLAB * r : SLAB * r + SLAB] for s in range(NZ)
            ]
            resp_full[2 * h + r] = jnp.concatenate(whole, axis=0).astype(BF16)

    unpack(0)
    for d in Z_ORDER:
        src = lax.rem(z + d, NZ)
        remote(
            table_got.at[src], table_got.at[src], table_s.at[0], table_r.at[src], p.z_peer(d, c)
        ).wait_recv()
    table[...] = table_got[...].reshape(N, N).T

    occ_gather.hand_on(1)
    occ_gather.hand_on(3)

    def pick(t, values):
        out = values[0]
        for i in range(1, 4):
            out = jnp.where(t == i, values[i], out)
        return out

    STEPS_X = ((0, 1, 0, 1), (3, 0, 3, 1), (3, 2, 0, 2), (1, 2, 3, 2))
    STEPS_Y = ((0, 0, 1, 1), (0, 3, 1, 3), (3, 0, 2, 1), (2, 3, 2, 2))

    def slots_of(t):
        out = []
        for q in range(4):
            dx = pick(t, [STEPS_X[i][q] for i in range(4)])
            dy = pick(t, [STEPS_Y[i][q] for i in range(4)])
            out.append(4 * mod4(y + dy) + mod4(x + dx))
        return out

    def pairs(h, t):
        orbitals = [occ_all[sl].reshape(N, N) for sl in slots_of(t)]
        which = [(r, q) for r in range(2) for q in range(4)]
        first = [
            jnp.dot(
                orbitals[q] * resp_full[2 * h + r], ct_ref[...], preferred_element_type=F32
            ).astype(BF16)
            for r, q in which
        ]
        weighted = [
            (jnp.dot(c_ref[...], f, preferred_element_type=F32) * table[...]).astype(BF16)
            for f in first
        ]
        third = [
            jnp.dot(ct_ref[...], w, preferred_element_type=F32).astype(BF16) for w in weighted
        ]
        for r in range(2):
            acc = total[r]
            for q in range(4):
                potential = jnp.dot(third[4 * r + q], c_ref[...], preferred_element_type=F32)
                acc = acc + orbitals[q].astype(F32) * potential
            total[r] = acc

    def rs_copy(h, d):
        to = lax.rem(z + d, NZ)
        return remote(
            rs_src.at[h, to],
            rs_got.at[h, z],
            rs_s.at[7 * h + d - 1],
            rs_r.at[8 * h + z],
            p.z_peer(d, c),
        )

    def reduce_start(h):
        for s in range(NZ):
            pair = [total[r, SLAB * s : SLAB * s + SLAB, :] for r in range(2)]
            rs_src[h, s] = (jnp.concatenate(pair, axis=0) * (1.0 / BANDS)).astype(BF16)
        for d in Z_ORDER:
            rs_copy(h, d).start()
        for r in range(2):
            start = pl.multiple_of(SLAB * z, 8)
            exch_own[2 * h + r] = total[r, pl.ds(start, SLAB), :] * (1.0 / BANDS)

    def reduce_finish(h):
        acc = [exch_own[2 * h + r] for r in range(2)]
        for d in Z_ORDER:
            src = lax.rem(z + d, NZ)
            remote(
                rs_got.at[h, src],
                rs_got.at[h, src],
                rs_s.at[0],
                rs_r.at[8 * h + src],
                p.z_peer(d, c),
            ).wait_recv()
            got = rs_got[h, src].astype(F32)
            for r in range(2):
                acc[r] = acc[r] + got[SLAB * r : SLAB * r + SLAB]
        for r in range(2):
            exch_own[2 * h + r] = acc[r]
        exch_wire[h] = jnp.concatenate(acc, axis=0).astype(BF16)

    total[...] = jnp.zeros_like(total)

    def step_one(t, carry):
        @pl.when(t == 1)
        def _():
            occ_gather.hand_on(2)

        for sl in slots_of(t):
            occ_gather.wait_sib(sl)
        pairs(0, t)
        return carry

    lax.fori_loop(0, 4, step_one, 0)
    reduce_start(0)
    resp_gather.start()
    unpack(1)
    total[...] = jnp.zeros_like(total)

    def step_two(t, carry):
        @pl.when(t == 1)
        def _():
            resp_gather.forward()

        pairs(1, t)
        return carry

    lax.fori_loop(0, 4, step_two, 0)
    reduce_start(1)

    for e in (1, 3, 2):
        resp_gather.hand_on(e)
    for k in range(2):
        remote(
            halo_src.at[k], halo_got.at[k], halo_s.at[k], halo_r.at[k], p.z_peer((7, 1)[k], c)
        ).wait_recv()
    for j in range(8):
        band = resp_ref[j].astype(F32)
        above = jnp.concatenate([halo_got[0, j : j + 1, :], band[: SLAB - 1]], axis=0)
        below = jnp.concatenate([band[1:], halo_got[1, j : j + 1, :]], axis=0)
        left = jnp.concatenate([band[:, N - 1 :], band[:, : N - 1]], axis=1)
        right = jnp.concatenate([band[:, 1:], band[:, :1]], axis=1)
        value = 0.5 * (4.0 * band - ((above + below) + left + right))
        value = value + (local_ref[...] - energy_ref[j]) * band
        weights = [jnp.where(index_ref[j] == k, 1.0, 0.0) for k in range(3)]
        perturb = weights[0] * field_ref[0] + weights[1] * field_ref[1] + weights[2] * field_ref[2]
        res_ref[j] = value + perturb * ground_ref[j].astype(F32)

    row = lax.broadcasted_iota(jnp.int32, (256, BANDS), 0)
    col = lax.broadcasted_iota(jnp.int32, (256, BANDS), 1)
    chip, member = row // 16, row % 8
    chip_x, chip_y = chip % 4, chip // 4
    natural = 32 * chip_x + 16 * (chip_y % 2) + 8 * (member // 4) + 4 * (chip_y // 2) + member % 4
    spread[...] = jnp.where(natural == col, 1.0, 0.0).astype(BF16)
    parity = (lax.broadcasted_iota(jnp.int32, (8, 256), 1) // 8) % 2

    for s in range(16):
        resp_gather.wait_sib(s)

    reduce_finish(0)
    reduce_finish(1)

    def sib_exch(h):
        return remote(exch_wire.at[h], resp_sib.at[2 + h], sib_s.at[2 + h], sib_r.at[2 + h], p.sibling)

    for h in range(2):
        sib_exch(h).start()

    zero = jnp.zeros((SLAB, N), F32)
    own_part = slab_of(lambda h: exch_wire[h])
    arrange(by_core(own_part, lambda r: zero))
    left_rows = rows32[...].reshape(N, N).astype(BF16)
    part = jnp.zeros((16, 256), F32)
    for a in range(SLAB // 2):
        bands = resp_all[:, a // 6, 16 * (a % 6) : 16 * (a % 6) + 16, :].reshape(256, N)
        part = part + lax.dot_general(
            left_rows[16 * a : 16 * a + 16],
            bands,
            (((1,), (1,)), ((), ())),
            preferred_element_type=F32,
        )
    folded = jnp.where(parity == 0, part[:8], part[8:])
    pieces = jnp.concatenate(split_bf16(folded), axis=0).astype(BF16)
    pieces = jnp.dot(pieces, spread[...], preferred_element_type=F32)
    gram_z[2 * z + c] = (pieces[:8] + pieces[8:16] + pieces[16:24]) * (1.0 / (N * N))

    z_line = [(d, k) for d in Z_ORDER for k in (0, 1)] + [(0, 1)]

    def line_core(k):
        return (1 - k) * c + k * (1 - c)

    def gram_copy(i):
        d, k = z_line[i]
        mine_slot = gram_z.at[2 * z + c]
        return remote(
            mine_slot, mine_slot, gz_s.at[i], gz_r.at[2 * z + c], p.z_peer(d, line_core(k))
        )

    for i in range(len(z_line)):
        gram_copy(i).start()

    for h in range(2):
        sib_exch(h).wait_recv()
    arrange(by_core(own_part, slab_of(lambda h: resp_sib[2 + h])))
    exch_all[own, c] = rows_half()
    exch_gather.start()

    for d, k in z_line:
        src = 2 * lax.rem(z + d, NZ) + line_core(k)
        slot = gram_z.at[src]
        remote(slot, slot, gz_s.at[0], gz_r.at[src], p.z_peer(d, line_core(k))).wait_recv()
    summed = gram_z[0]
    for i in range(1, 2 * NZ):
        summed = summed + gram_z[i]
    gram_xy[y, x] = summed

    def gx_copy(d):
        slot = gram_xy.at[y, x]
        return remote(slot, slot, gx_s.at[d - 1], gx_r.at[x], p.dev(mod4(x + d), y, z, c))

    def gy_copy(d):
        slot = gram_xy.at[y]
        return remote(slot, slot, gy_s.at[d - 1], gy_r.at[y], p.dev(x, mod4(y + d), z, c))

    for d in (1, 3, 2):
        gx_copy(d).start()
    exch_gather.forward()
    for d in (1, 3, 2):
        src = mod4(x + d)
        slot = gram_xy.at[y, src]
        remote(slot, slot, gx_s.at[0], gx_r.at[src], p.dev(src, y, z, c)).wait_recv()
    for d in (1, 3, 2):
        gy_copy(d).start()
    for e in (1, 3, 2):
        exch_gather.hand_on(e)
    for d in (1, 3, 2):
        src = mod4(y + d)
        slot = gram_xy.at[src]
        remote(slot, slot, gy_s.at[0], gy_r.at[src], p.dev(x, src, z, c)).wait_recv()

    for i in range(32):
        n_x, n_lo, n_c, n_g = i // 8, (i // 4) % 2, (i // 2) % 2, i % 2
        gram_full[4 * i : 4 * i + 4, :] = gram_xy[2 * n_g + n_lo, n_x, 4 * n_c : 4 * n_c + 4, :]
    gram = gram_full[...]
    gram_full[...] = inverse_factor(0.5 * (gram + gram.T))
    inverse = gram_full[pl.ds(pl.multiple_of(8 * p.b, 8), 8), :]

    for s in range(16):
        exch_gather.wait_sib(s)

    for half in range(2):
        slot = 4 * (2 * half + p.y_lo) + x
        rows32[...] = exch_all[slot].reshape(SLAB, 8, N).astype(F32)
        for r in range(4):
            value = jnp.where(c == 0, rows32[:, r, :], rows32[:, 4 + r, :])
            res_ref[4 * half + r] = res_ref[4 * half + r] - EXCHANGE_FRACTION * value

    pieces = jnp.concatenate(split_bf16(inverse), axis=0).astype(BF16)
    wide = lax.dot_general(
        pieces, spread[...], (((1,), (1,)), ((), ())), preferred_element_type=F32
    )
    parity = jnp.concatenate([parity] * 3, axis=0)
    left = jnp.concatenate(
        [jnp.where(parity == 0, wide, 0.0), jnp.where(parity == 1, wide, 0.0)], axis=0
    ).astype(BF16)
    for a in range(SLAB // 2):
        vectors = exch_all[:, a // 6, 16 * (a % 6) : 16 * (a % 6) + 16, :].reshape(256, N)
        out = jnp.dot(left, vectors, preferred_element_type=F32)
        for k in range(2):
            o = out[24 * k : 24 * k + 24]
            proj32[:, 2 * a + k, :] = (o[16:24] + o[8:16]) + o[:8]
    for j in range(8):
        proj_ref[j] = proj32[j].astype(BF16)

    for r in range(4):
        @pl.when(jnp.logical_not(mine(r)))
        def _():
            occ_out(r).wait_send()

    for d in range(1, NZ):
        table_copy(d).wait_send()
        for h in range(2):
            resp_copy(h, d).wait_send()
            rs_copy(h, d).wait_send()
    for h in range(2):
        sib_resp(h).wait_send()
        sib_exch(h).wait_send()
        halo_copy(h).wait_send()
    for i in range(len(z_line)):
        gram_copy(i).wait_send()
    for d in (1, 2, 3):
        gx_copy(d).wait_send()
        gy_copy(d).wait_send()
    for gather in (occ_gather, resp_gather, exch_gather):
        gather.finish()


def on_device(*arguments):
    table = cosine_table(N)
    vmem = pl.BlockSpec(memory_space=pltpu.VMEM)
    smem = pl.BlockSpec(memory_space=pltpu.SMEM)
    dma = lambda n: pltpu.SemaphoreType.DMA((n,))
    scratch = [
        pltpu.VMEM((4, SLAB, N), F32),
        pltpu.VMEM((4, SLAB, N), F32),
        pltpu.VMEM((2, NZ, 2 * SLAB, N), BF16),
        pltpu.VMEM((4, 2 * SLAB, N), BF16),
        pltpu.VMEM((4, N, N), BF16),
        pltpu.VMEM((NZ, SLAB, N), F32),
        pltpu.VMEM((N, N), F32),
        pltpu.VMEM((2, 8, N), F32),
        pltpu.VMEM((2, 8, N), F32),
        pltpu.VMEM((16, 2, HALF, N), BF16),
        pltpu.VMEM((16, 2, HALF, N), BF16),
        pltpu.VMEM((16, 2, HALF, N), BF16),
        pltpu.VMEM((2, N, N), F32),
        pltpu.VMEM((2, NZ, 2 * SLAB, N), BF16),
        pltpu.VMEM((2, NZ, 2 * SLAB, N), BF16),
        pltpu.VMEM((SLAB, 8, N), F32),
        pltpu.VMEM((4, SLAB, N), F32),
        pltpu.VMEM((2, 2 * SLAB, N), BF16),
        pltpu.VMEM((2 * NZ, 8, BANDS), F32),
        pltpu.VMEM((4, 4, 8, BANDS), F32),
        pltpu.VMEM((BANDS, BANDS), F32),
        pltpu.VMEM((256, BANDS), BF16),
        pltpu.VMEM((8, SLAB, N), F32),
    ]
    counts = [4, 4, 14, 16, 4, 4, 7, 8, 2, 2, 14, 16, 15, 16, 3, 4, 3, 4] + [3, 12, 16, 16, 16] * 3
    scratch += [dma(n) for n in counts]
    return pl.pallas_call(
        kernel,
        out_shape=(
            jax.ShapeDtypeStruct((8, SLAB, N), BF16),
            jax.ShapeDtypeStruct((8, SLAB, N), F32),
        ),
        in_specs=[vmem, vmem, vmem, smem, smem, vmem, vmem, vmem, vmem, vmem],
        out_specs=(vmem, vmem),
        scratch_shapes=scratch,
        compiler_params=pltpu.CompilerParams(
            collective_id=0, has_side_effects=True, vmem_limit_bytes=48 << 20
        ),
        cost_estimate=pl.CostEstimate(
            flops=4 * 64 * 2 * N**3, bytes_accessed=4 << 20, transcendentals=0
        ),
    )(*arguments, jnp.asarray(table), jnp.asarray(np.ascontiguousarray(table.T)))


def solution(mesh):
    return jax.shard_map(
        on_device,
        mesh=mesh,
        in_specs=(
            P(("grp", "band"), "ga", None),
            P("band", "ga", None),
            P("band", "ga", None),
            P("band"),
            P("band"),
            P("ga", None),
            P(None, "ga", None),
            P(None, "ga"),
        ),
        out_specs=(P("band", "ga", None), P("band", "ga", None)),
        check_vma=False,
    )
```

time: 865 us -> 76.7 us (0.09); the launches traced: 852 us -> 76 us
  blocking collectives: 278 us -> 0 us
  local copies, waits for them, and re-layouts: 206 us -> 7.89 us
  starting transfers between devices: 165 us -> 0 us
  waiting for transfers between devices: 77 us -> 0 us
  Pallas kernels: 0 us -> 67.4 us
  matrix products: 65 us -> 0 us
  other arithmetic: 42.7 us -> 0 us
  between operations: 16 us -> 0.67 us
    all_to_all x17 -> x0, blocking collectives: 243 us -> none  [the longest x16 231 us: pair_field(): lax.all_to_all(first, 'ga', split_axis=2, concat_axis=1, tiled=True)]
    ppermute x17 -> x0, starting transfers between devices: 113 us -> none  [the longest x15 110 us: passed_along(): lax.ppermute(x, axis, [(i, (i + by) % devices) for i in range(devices)])]
    all_to_all x48 -> x0, local copies, waits for them, and re-layouts: 97.1 us -> none  [the longest x32 56.8 us: pair_field(): lax.all_to_all(first, 'ga', split_axis=2, concat_axis=1, tiled=True)]
    pallas_call x0 -> x1, Pallas kernels: none -> 67.4 us  [on_device(): pl.pallas_call(kernel, out_shape=(jax.ShapeDtypeStruct((8, SLAB, N), BF16...]
    dot_general x51 -> x0, matrix products: 64.8 us -> none  [the longest x16 29 us: pair_field(): jnp.einsum('ka,pkb->pab', table_one, weighted, preferred_element_type=jnp...]
    while x105 -> x0, local copies, waits for them, and re-layouts: 60.9 us -> none
    all_to_all x15 -> x0, starting transfers between devices: 51.3 us -> none  [pair_field(): lax.all_to_all(third, 'ga', split_axis=1, concat_axis=2, tiled=True)]
    psum x1 -> x0, waiting for transfers between devices: 38.8 us -> none  [on_device(): exchange = lax.psum(total, 'grp')]
  transfers between devices with their start and end apart: 35 -> 0, of which waited for: 18 -> 0; matrix products, arithmetic and copies ran while one was open for 12% -> 0% of each run, Pallas kernels for 0% -> 0%
where the time goes in v1:
time: 76.7 us; the launch traced here: 76 us
  Pallas kernels  67.4 us (88%)
  local copies, waits for them, and re-layouts  7.89 us (10%)
    pallas_call x1, Pallas kernels, on_device(): pl.pallas_call(kernel, out_shape=(jax.ShapeDtypeStruct((8, SLAB, N), BF16...  67.4 us
    unnamed x21, local copies, waits for them, and re-layouts  7.89 us

profile of v1, /device:TPU:1, one launch (start us, length us, event | category | flops | bytes accessed | tf_op | source)
XLA Modules:
  0.0 76.0 jit_solution(1945817029622938059)
XLA Ops:
  0.6 0.0 copy-start.4
  0.6 0.0 copy-start
  0.7 0.9 %copy.12.table_ref = f32[192,24]{1,0:T(8,128)S(1)} copy(f32[192,24]{0,1:T(8,128)} %param.17) | data formatting | bytes 36864 | tf_op args[7]
  1.5 0.0 copy-done.4
  1.5 0.0 copy-done
  1.6 0.0 copy-start.1
  1.6 0.9 %copy-done.1 = bf16[8,24,192]{2,1,0:T(8,128)(2,1)S(1)} copy-done((bf16[8,24,192]{2,1,0:T(8,128)(2,1)S(1)}, bf16[8,24,192]{2,1,0:T(8,128)(2,1)}, u32[]{:S(2)}) %copy-start.1) | copy-done | bytes 73752
  2.5 0.0 copy-start.2
  2.5 0.9 %copy-done.2 = f32[3,24,192]{2,1,0:T(8,128)S(1)} copy-done((f32[3,24,192]{2,1,0:T(8,128)S(1)}, f32[3,24,192]{2,1,0:T(8,128)}, u32[]{:S(2)}) %copy-start.2) | copy-done | bytes 55320
  3.3 0.0 copy-start.3
  3.3 0.8 %copy-done.3 = bf16[4,24,192]{2,1,0:T(8,128)(2,1)S(1)} copy-done((bf16[4,24,192]{2,1,0:T(8,128)(2,1)S(1)}, bf16[4,24,192]{2,1,0:T(8,128)(2,1)}, u32[]{:S(2)}) %copy-start.3) | copy-done | bytes 36888
  4.1 0.0 copy-start.5
  4.1 0.7 copy-done.5
  4.8 0.0 copy-start.6
  4.8 0.7 copy-done.6
  5.4 0.0 copy-start.7
  5.4 0.9 %copy-done.7 = bf16[192,192]{1,0:T(8,128)(2,1)S(1)} copy-done((bf16[192,192]{1,0:T(8,128)(2,1)S(1)}, bf16[192,192]{1,0:T(8,128)(2,1)}, u32[]{:S(2)}) %copy-start.7) | copy-done | bytes 73752
  6.3 0.0 copy-start.8
  6.3 0.9 %copy-done.8 = bf16[192,192]{1,0:T(8,128)(2,1)S(1)} copy-done((bf16[192,192]{1,0:T(8,128)(2,1)S(1)}, bf16[192,192]{1,0:T(8,128)(2,1)}, u32[]{:S(2)}) %copy-start.8) | copy-done | bytes 73752
  7.2 67.4 %shard_map.113 = (bf16[8,24,192]{2,1,0:T(8,128)(2,1)S(1)}, f32[8,24,192]{2,1,0:T(8,128)S(1)}) custom-call(bf16[4,24,192]{2,1,0:T(8,128)(2,1)S(1)} %copy-done.3, bf16[8,24,192]{2,1,0:T(8,128)(2,1)S(1)} %copy-done, bf16[8,24,192]{2,1,0:T(8,128)(2,1)S(1)} %copy-done.1, s32[8]{0:T(128)S(1)} %copy-done.5, f32[8]{0:T(128)S(1)} %copy-done.6, ...), custom_call_target="tpu_custom_call" | custom-call | flops 3623878656 | bytes 4194304 | tf_op jit(solution)/shard_map/pallas_call | solution.py:725
  74.7 0.6 copy.15
  75.3 0.7 copy.16
Async XLA Ops:
  0.6 0.9 %copy-start.4 = (f32[24,192]{1,0:T(8,128)S(1)}, f32[24,192]{1,0:T(8,128)}, u32[]{:S(2)}) copy-start(f32[24,192]{1,0:T(8,128)} %local_ref.1) | copy-start | bytes 55300
  0.6 0.9 %copy-start = (bf16[8,24,192]{2,1,0:T(8,128)(2,1)S(1)}, bf16[8,24,192]{2,1,0:T(8,128)(2,1)}, u32[]{:S(2)}) copy-start(bf16[8,24,192]{2,1,0:T(8,128)(2,1)} %resp_ref.1) | copy-start | bytes 221188
  1.6 0.9 %copy-start.1 = (bf16[8,24,192]{2,1,0:T(8,128)(2,1)S(1)}, bf16[8,24,192]{2,1,0:T(8,128)(2,1)}, u32[]{:S(2)}) copy-start(bf16[8,24,192]{2,1,0:T(8,128)(2,1)} %ground_ref.1) | copy-start | bytes 221188
  2.5 0.9 %copy-start.2 = (f32[3,24,192]{2,1,0:T(8,128)S(1)}, f32[3,24,192]{2,1,0:T(8,128)}, u32[]{:S(2)}) copy-start(f32[3,24,192]{2,1,0:T(8,128)} %field_ref.1) | copy-start | bytes 165892
  3.3 0.8 %copy-start.3 = (bf16[4,24,192]{2,1,0:T(8,128)(2,1)S(1)}, bf16[4,24,192]{2,1,0:T(8,128)(2,1)}, u32[]{:S(2)}) copy-start(bf16[4,24,192]{2,1,0:T(8,128)(2,1)} %occ_ref.1) | copy-start | bytes 110596
  4.1 0.7 copy-start.5
  4.8 0.7 copy-start.6
  5.4 0.9 %copy-start.7 = (bf16[192,192]{1,0:T(8,128)(2,1)S(1)}, bf16[192,192]{1,0:T(8,128)(2,1)}, u32[]{:S(2)}) copy-start(bf16[192,192]{1,0:T(8,128)(2,1)} %constant.5.clone.ct_ref) | copy-start | bytes 221188
  6.3 0.9 %copy-start.8 = (bf16[192,192]{1,0:T(8,128)(2,1)S(1)}, bf16[192,192]{1,0:T(8,128)(2,1)}, u32[]{:S(2)}) copy-start(bf16[192,192]{1,0:T(8,128)(2,1)} %constant.4.clone.c_ref) | copy-start | bytes 221188

commit v2 on v1

--- a/solution.py
+++ b/solution.py
@@ -28,13 +28,41 @@
     return (factor * np.cos(angle)).astype(ml_dtypes.bfloat16)
 
 
-def inverse_factor(gram):
+def pack_one(slab):
+    ends = slab[:, 128:]
+    ends = jnp.concatenate(
+        [
+            jnp.concatenate([ends[:8], ends[8:16]], axis=1),
+            jnp.concatenate([ends[16:], jnp.zeros((8, 64), F32)], axis=1),
+        ],
+        axis=0,
+    )
+    unused = jnp.zeros((WIRE_ONE - SLAB - 16, 128), F32)
+    return jnp.concatenate([slab[:, :128], ends, unused], axis=0).astype(BF16)
+
+
+def unpack_one(wire):
+    value = wire.astype(F32)
+    ends = value[SLAB : SLAB + 16]
+    ends = jnp.concatenate([ends[:8, :64], ends[:8, 64:], ends[8:, :64]], axis=0)
+    return [jnp.concatenate([value[:SLAB], ends], axis=1)]
+
+
+def tree_sum(terms):
+    while len(terms) > 1:
+        terms = [a + b for a, b in zip(terms[::2], terms[1::2])] + terms[len(terms) & ~1 :]
+    return terms[0]
+
+
+def inverse_factor(gram, halfway):
     lane = lax.broadcasted_iota(jnp.int32, (8, BANDS), 1)
     sub = lax.broadcasted_iota(jnp.int32, (8, BANDS), 0)
     count = BANDS // 8
     blocks = [gram[8 * i : 8 * i + 8, :] for i in range(count)]
     done = []
     for b in range(count):
+        if b == 9:
+            halfway()
         k0 = 8 * b
         inside = (lane >= k0) & (lane < k0 + 8)
         rows = [jnp.broadcast_to(blocks[b][t : t + 1, :], (8, BANDS)) for t in range(8)]
@@ -55,19 +83,12 @@
         for s in range(8):
             inv[s][s] = rinv[s]
             for t in range(s + 1, 8):
-                acc = low[t][s] * inv[s][s]
-                for u in range(s + 1, t):
-                    acc = acc + low[t][u] * inv[u][s]
+                acc = tree_sum([low[t][u] * inv[u][s] for u in range(s, t)])
                 inv[t][s] = -(acc * rinv[t])
         unit = [
             jnp.where(lane == k0 + t, 1.0, jnp.where(inside, 0.0, rows[t])) for t in range(8)
         ]
-        panel = []
-        for t in range(8):
-            acc = inv[t][0] * unit[0]
-            for s in range(1, t + 1):
-                acc = acc + inv[t][s] * unit[s]
-            panel.append(acc)
+        panel = [tree_sum([inv[t][s] * unit[s] for s in range(t + 1)]) for t in range(8)]
         packed = panel[0]
         for t in range(1, 8):
             packed = jnp.where(sub == t, panel[t], packed)
@@ -77,12 +98,8 @@
                 jnp.broadcast_to(blocks[i][:, k0 + s : k0 + s + 1], (8, BANDS)) for s in range(8)
             ]
             new = jnp.where(inside, 0.0, blocks[i])
-            for t in range(8):
-                factor = inv[t][0] * column[0]
-                for s in range(1, t + 1):
-                    factor = factor + inv[t][s] * column[s]
-                new = new - factor * panel[t]
-            blocks[i] = new
+            factor = [tree_sum([inv[t][s] * column[s] for s in range(t + 1)]) for t in range(8)]
+            blocks[i] = new - tree_sum([factor[t] * panel[t] for t in range(8)])
     return jnp.concatenate(done, axis=0)
 
 
@@ -157,8 +174,8 @@
                 self.second_copy(d, e).start()
             self.sib_copy(d, 0).start()
 
-    def hand_on(self, e):
-        for d in (0, 1, 3, 2):
+    def hand_on(self, offsets):
+        for d, e in offsets:
             sl = self.slot(d, e)
             self.copy(
                 sl, self.place.c, self.s_first.at[0], self.r_ici.at[sl], self.peer(0, e)
@@ -211,10 +228,41 @@
     )
 
 
-Z_ORDER = (1, 7, 2, 6, 3, 5, 4)
+Z_ORDER = (4, 3, 5, 2, 6, 1, 7)
+NEAR = ((0, 1), (0, 3), (0, 2))
+LATE = ((1, 1), (1, 3), (3, 1), (3, 3), (1, 2), (2, 1), (3, 2), (2, 3), (2, 2))
+WIRE_ONE = 48
+WIRE = 80
+
+
+def pack(pair):
+    ends = jnp.concatenate([pair[:SLAB, 128:], pair[SLAB:, 128:]], axis=1)
+    unused = jnp.zeros((WIRE - 3 * SLAB, 128), F32)
+    return jnp.concatenate([pair[:, :128], ends, unused], axis=0).astype(BF16)
+
+
+def unpack(wire):
+    value = wire.astype(F32)
+    ends = value[2 * SLAB : 3 * SLAB]
+    return [
+        jnp.concatenate([value[:SLAB], ends[:, :64]], axis=1),
+        jnp.concatenate([value[SLAB : 2 * SLAB], ends[:, 64:]], axis=1),
+    ]
 
 
 def kernel(
+    occ_hbm,
+    resp_hbm,
+    ground_hbm,
+    index_hbm,
+    energy_hbm,
+    local_hbm,
+    field_hbm,
+    table_hbm,
+    c_hbm,
+    ct_hbm,
+    proj_ref,
+    res_ref,
     occ_ref,
     resp_ref,
     ground_ref,
@@ -222,11 +270,8 @@
     energy_ref,
     local_ref,
     field_ref,
-    table_ref,
     c_ref,
     ct_ref,
-    proj_ref,
-    res_ref,
     occ_src,
     occ_got,
     resp_got,
@@ -242,6 +287,8 @@
     total,
     rs_src,
     rs_got,
+    rs_src_one,
+    rs_got_one,
     rows32,
     exch_own,
     exch_wire,
@@ -256,33 +303,55 @@
     z, c, x, y, g = p.z, p.c, p.x, p.y, p.g
     sems = list(sems)
     take = lambda: sems.pop(0)
+    in_s = take()
     occ_s, occ_r = take(), take()
     resp_s, resp_r = take(), take()
     sib_s, sib_r = take(), take()
     table_s, table_r = take(), take()
+    table_sib_s, table_sib_r = take(), take()
     halo_s, halo_r = take(), take()
     rs_s, rs_r = take(), take()
     gz_s, gz_r = take(), take()
-    gx_s, gx_r = take(), take()
-    gy_s, gy_r = take(), take()
+    gp_s, gp_r = take(), take()
     occ_gather = PlaneGather(p, occ_all, *[take() for _ in range(5)])
     resp_gather = PlaneGather(p, resp_all, *[take() for _ in range(5)])
     exch_gather = PlaneGather(p, exch_all, *[take() for _ in range(5)])
 
+    loads = [
+        pltpu.make_async_copy(src, dst, in_s.at[i])
+        for i, (src, dst) in enumerate(
+            (
+                (occ_hbm, occ_ref),
+                (resp_hbm, resp_ref),
+                (table_hbm, table_got.at[z]),
+                (c_hbm, c_ref),
+                (ct_hbm, ct_ref),
+                (ground_hbm, ground_ref),
+                (field_hbm, field_ref),
+                (local_hbm, local_ref),
+                (index_hbm, index_ref),
+                (energy_hbm, energy_ref),
+            )
+        )
+    ]
+    for load in loads:
+        load.start()
+
     barrier = pltpu.get_barrier_semaphore()
     peers = [p.z_peer(d, k) for d in range(1, NZ) for k in (0, 1)]
     peers += [p.sibling]
-    peers += [p.dev(mod4(x + d), y, z, c) for d in (1, 2, 3)]
-    peers += [p.dev(x, mod4(y + d), z, c) for d in (1, 2, 3)]
+    plane = [(d, e) for d in (2, 1, 3, 0) for e in (2, 1, 3, 0) if (d, e) != (0, 0)]
+    peers += [p.dev(mod4(x + d), mod4(y + e), z, c) for d, e in plane]
     for peer in peers:
         pl.semaphore_signal(barrier, inc=1, device_id=peer, device_id_type=MESH)
 
-    table_got[z] = table_ref[...].T
+    for load in loads[:3]:
+        load.wait()
     for r in range(4):
-        occ_src[r] = occ_ref[r].astype(F32)
+        occ_src[r] = pack_one(occ_ref[r].astype(F32))
     for h in range(2):
         pair = [resp_ref[4 * g + 2 * h + r].astype(F32) for r in range(2)]
-        resp_got[h, z] = jnp.concatenate(pair, axis=0).astype(BF16)
+        resp_got[h, z] = pack(jnp.concatenate(pair, axis=0))
     edge = [resp_ref[j].astype(F32) for j in range(8)]
     halo_src[0] = jnp.concatenate([e[SLAB - 1 : SLAB] for e in edge], axis=0)
     halo_src[1] = jnp.concatenate([e[0:1] for e in edge], axis=0)
@@ -321,8 +390,35 @@
         def _():
             occ_got[r] = occ_src[r]
 
-    def table_copy(d):
-        return remote(table_got.at[z], table_got.at[z], table_s.at[d - 1], table_r.at[z], p.z_peer(d, c))
+    def table_copy(i):
+        d = 2 * i + 2 - c
+        return remote(
+            table_got.at[z], table_got.at[z], table_s.at[i], table_r.at[z], p.z_peer(d, c)
+        )
+
+    def table_on(i):
+        src = lax.rem(z + NZ - (2 * i + 2 - c), NZ)
+        slot = table_got.at[src]
+        return remote(slot, slot, table_sib_s.at[i], table_sib_r.at[src], p.sibling)
+
+    def table_wait(i):
+        src = lax.rem(z + NZ - (2 * i + 2 - c), NZ)
+        slot = table_got.at[src]
+        remote(slot, slot, table_s.at[0], table_r.at[src], p.sibling).wait_recv()
+        table_on(i).start()
+
+    def table_wait_sib(i):
+        src = lax.rem(z + NZ - (2 * i + 1 + c), NZ)
+        slot = table_got.at[src]
+        remote(slot, slot, table_sib_s.at[0], table_sib_r.at[src], p.sibling).wait_recv()
+
+    def for_table(core, act):
+        for i in range(3):
+            act(i)
+
+        @pl.when(core == 1)
+        def _():
+            act(3)
 
     def resp_copy(h, d):
         return remote(
@@ -351,10 +447,9 @@
             halo_src.at[k], halo_got.at[k], halo_s.at[k], halo_r.at[k], p.z_peer((1, 7)[k], c)
         )
 
+    for_table(c, lambda i: table_copy(i).start())
     for d in Z_ORDER:
         resp_copy(0, d).start()
-    for d in Z_ORDER:
-        table_copy(d).start()
     for d in Z_ORDER:
         resp_copy(1, d).start()
     for h in range(2):
@@ -368,7 +463,9 @@
             occ_in(q).wait_recv()
 
     own = 4 * y + x
-    occ_all[own, c] = jnp.concatenate([occ_got[q] for q in range(4)], axis=0).astype(BF16)
+    occ_all[own, c] = jnp.concatenate(
+        [unpack_one(occ_got[q])[0] for q in range(4)], axis=0
+    ).astype(BF16)
     occ_gather.start()
 
     def arrange(parts):
@@ -385,7 +482,7 @@
 
     def slab_of(ref):
         def part(r):
-            return ref(r // 2).astype(F32)[SLAB * (r % 2) : SLAB * (r % 2) + SLAB]
+            return unpack(ref(r // 2))[r % 2]
 
         return part
 
@@ -394,27 +491,23 @@
     arrange(by_core(slab_of(lambda h: resp_got[h, z]), slab_of(lambda h: resp_sib[h])))
     resp_all[own, c] = rows_half()
 
+    for load in loads[3:]:
+        load.wait()
+    for_table(c, table_wait)
     occ_gather.forward()
-
-    def unpack(h):
+    occ_gather.hand_on(NEAR)
+    for_table(1 - c, table_wait_sib)
+    table[...] = table_got[...].reshape(N, N).T
+
+    def whole_bands(h):
         for d in Z_ORDER:
             resp_wait(h, d)
+        parts = [unpack(resp_got[h, s]) for s in range(NZ)]
         for r in range(2):
-            whole = [
-                resp_got[h, s].astype(F32)[SLAB * r : SLAB * r + SLAB] for s in range(NZ)
-            ]
+            whole = [parts[s][r] for s in range(NZ)]
             resp_full[2 * h + r] = jnp.concatenate(whole, axis=0).astype(BF16)
 
-    unpack(0)
-    for d in Z_ORDER:
-        src = lax.rem(z + d, NZ)
-        remote(
-            table_got.at[src], table_got.at[src], table_s.at[0], table_r.at[src], p.z_peer(d, c)
-        ).wait_recv()
-    table[...] = table_got[...].reshape(N, N).T
-
-    occ_gather.hand_on(1)
-    occ_gather.hand_on(3)
+    whole_bands(0)
 
     def pick(t, values):
         out = values[0]
@@ -422,8 +515,8 @@
             out = jnp.where(t == i, values[i], out)
         return out
 
-    STEPS_X = ((0, 1, 0, 1), (3, 0, 3, 1), (3, 2, 0, 2), (1, 2, 3, 2))
-    STEPS_Y = ((0, 0, 1, 1), (0, 3, 1, 3), (3, 0, 2, 1), (2, 3, 2, 2))
+    STEPS_X = ((0, 1, 0, 3), (0, 2, 0, 1), (1, 3, 3, 1), (2, 3, 2, 2))
+    STEPS_Y = ((0, 0, 1, 0), (3, 0, 2, 1), (3, 1, 3, 2), (1, 2, 3, 2))
 
     def slots_of(t):
         out = []
@@ -433,13 +526,11 @@
             out.append(4 * mod4(y + dy) + mod4(x + dx))
         return out
 
-    def pairs(h, t):
-        orbitals = [occ_all[sl].reshape(N, N) for sl in slots_of(t)]
-        which = [(r, q) for r in range(2) for q in range(4)]
+    def pairs(slots, bands):
+        orbitals = [occ_all[sl].reshape(N, N) for sl in slots]
+        which = [(r, q) for r in bands for q in range(len(slots))]
         first = [
-            jnp.dot(
-                orbitals[q] * resp_full[2 * h + r], ct_ref[...], preferred_element_type=F32
-            ).astype(BF16)
+            jnp.dot(orbitals[q] * resp_full[r], ct_ref[...], preferred_element_type=F32).astype(BF16)
             for r, q in which
         ]
         weighted = [
@@ -449,82 +540,91 @@
         third = [
             jnp.dot(ct_ref[...], w, preferred_element_type=F32).astype(BF16) for w in weighted
         ]
-        for r in range(2):
+        for r in bands:
             acc = total[r]
-            for q in range(4):
-                potential = jnp.dot(third[4 * r + q], c_ref[...], preferred_element_type=F32)
-                acc = acc + orbitals[q].astype(F32) * potential
+            for i, (band, q) in enumerate(which):
+                if band == r:
+                    potential = jnp.dot(third[i], c_ref[...], preferred_element_type=F32)
+                    acc = acc + orbitals[q].astype(F32) * potential
             total[r] = acc
+
+    groups = ((0, 1), (2,), (3,))
+
+    def rs_refs(h):
+        if h == 0:
+            return rs_src, rs_got
+        return rs_src_one.at[h - 1], rs_got_one.at[h - 1]
 
     def rs_copy(h, d):
         to = lax.rem(z + d, NZ)
+        src, dst = rs_refs(h)
         return remote(
-            rs_src.at[h, to],
-            rs_got.at[h, z],
-            rs_s.at[7 * h + d - 1],
-            rs_r.at[8 * h + z],
-            p.z_peer(d, c),
+            src.at[to], dst.at[z], rs_s.at[7 * h + d - 1], rs_r.at[8 * h + z], p.z_peer(d, c)
         )
 
     def reduce_start(h):
+        src, _ = rs_refs(h)
         for s in range(NZ):
-            pair = [total[r, SLAB * s : SLAB * s + SLAB, :] for r in range(2)]
-            rs_src[h, s] = (jnp.concatenate(pair, axis=0) * (1.0 / BANDS)).astype(BF16)
+            out = [total[r, SLAB * s : SLAB * s + SLAB, :] * (1.0 / BANDS) for r in groups[h]]
+            src[s] = pack(jnp.concatenate(out, axis=0)) if h == 0 else pack_one(out[0])
         for d in Z_ORDER:
             rs_copy(h, d).start()
-        for r in range(2):
-            start = pl.multiple_of(SLAB * z, 8)
-            exch_own[2 * h + r] = total[r, pl.ds(start, SLAB), :] * (1.0 / BANDS)
+        start = pl.multiple_of(SLAB * z, 8)
+        for r in groups[h]:
+            exch_own[r] = total[r, pl.ds(start, SLAB), :] * (1.0 / BANDS)
 
     def reduce_finish(h):
-        acc = [exch_own[2 * h + r] for r in range(2)]
+        _, dst = rs_refs(h)
+        acc = [exch_own[r] for r in groups[h]]
         for d in Z_ORDER:
             src = lax.rem(z + d, NZ)
-            remote(
-                rs_got.at[h, src],
-                rs_got.at[h, src],
-                rs_s.at[0],
-                rs_r.at[8 * h + src],
-                p.z_peer(d, c),
-            ).wait_recv()
-            got = rs_got[h, src].astype(F32)
-            for r in range(2):
-                acc[r] = acc[r] + got[SLAB * r : SLAB * r + SLAB]
-        for r in range(2):
-            exch_own[2 * h + r] = acc[r]
-        exch_wire[h] = jnp.concatenate(acc, axis=0).astype(BF16)
+            slot = dst.at[src]
+            remote(slot, slot, rs_s.at[0], rs_r.at[8 * h + src], p.z_peer(d, c)).wait_recv()
+            got = unpack(dst[src]) if h == 0 else unpack_one(dst[src])
+            acc = [a + b for a, b in zip(acc, got)]
+        for r, a in zip(groups[h], acc):
+            exch_own[r] = a
 
     total[...] = jnp.zeros_like(total)
 
     def step_one(t, carry):
+        @pl.when(t == 3)
+        def _():
+            resp_gather.start()
+
+        for sl in slots_of(t):
+            occ_gather.wait_sib(sl)
+        pairs(slots_of(t), groups[0])
+
+        @pl.when(t == 0)
+        def _():
+            occ_gather.hand_on(LATE[:4])
+
         @pl.when(t == 1)
         def _():
-            occ_gather.hand_on(2)
-
-        for sl in slots_of(t):
-            occ_gather.wait_sib(sl)
-        pairs(0, t)
+            occ_gather.hand_on(LATE[4:])
+
         return carry
 
     lax.fori_loop(0, 4, step_one, 0)
     reduce_start(0)
-    resp_gather.start()
-    unpack(1)
-    total[...] = jnp.zeros_like(total)
-
-    def step_two(t, carry):
-        @pl.when(t == 1)
-        def _():
-            resp_gather.forward()
-
-        pairs(1, t)
-        return carry
-
-    lax.fori_loop(0, 4, step_two, 0)
+    whole_bands(1)
+
+    def later_step(bands):
+        def step(t, carry):
+            pairs([8 * t + q for q in range(8)], bands)
+            return carry
+
+        return step
+
+    lax.fori_loop(0, 2, later_step(groups[1]), 0)
     reduce_start(1)
-
-    for e in (1, 3, 2):
-        resp_gather.hand_on(e)
+    resp_gather.forward()
+    resp_gather.hand_on(NEAR)
+    lax.fori_loop(0, 2, later_step(groups[2]), 0)
+    reduce_start(2)
+
+    resp_gather.hand_on(LATE)
     for k in range(2):
         remote(
             halo_src.at[k], halo_got.at[k], halo_s.at[k], halo_r.at[k], p.z_peer((7, 1)[k], c)
@@ -552,14 +652,18 @@
     for s in range(16):
         resp_gather.wait_sib(s)
 
-    reduce_finish(0)
-    reduce_finish(1)
-
     def sib_exch(h):
         return remote(exch_wire.at[h], resp_sib.at[2 + h], sib_s.at[2 + h], sib_r.at[2 + h], p.sibling)
 
-    for h in range(2):
+    def sib_exch_start(h):
+        exch_wire[h] = pack(jnp.concatenate([exch_own[2 * h], exch_own[2 * h + 1]], axis=0))
         sib_exch(h).start()
+
+    reduce_finish(0)
+    sib_exch_start(0)
+    reduce_finish(1)
+    reduce_finish(2)
+    sib_exch_start(1)
 
     zero = jnp.zeros((SLAB, N), F32)
     own_part = slab_of(lambda h: exch_wire[h])
@@ -609,35 +713,30 @@
         summed = summed + gram_z[i]
     gram_xy[y, x] = summed
 
-    def gx_copy(d):
+    def gram_plane(i):
+        d, e = plane[i]
         slot = gram_xy.at[y, x]
-        return remote(slot, slot, gx_s.at[d - 1], gx_r.at[x], p.dev(mod4(x + d), y, z, c))
-
-    def gy_copy(d):
-        slot = gram_xy.at[y]
-        return remote(slot, slot, gy_s.at[d - 1], gy_r.at[y], p.dev(x, mod4(y + d), z, c))
-
-    for d in (1, 3, 2):
-        gx_copy(d).start()
+        device = p.dev(mod4(x + d), mod4(y + e), z, c)
+        return remote(slot, slot, gp_s.at[i], gp_r.at[own], device)
+
+    for i in range(len(plane)):
+        gram_plane(i).start()
     exch_gather.forward()
-    for d in (1, 3, 2):
-        src = mod4(x + d)
-        slot = gram_xy.at[y, src]
-        remote(slot, slot, gx_s.at[0], gx_r.at[src], p.dev(src, y, z, c)).wait_recv()
-    for d in (1, 3, 2):
-        gy_copy(d).start()
-    for e in (1, 3, 2):
-        exch_gather.hand_on(e)
-    for d in (1, 3, 2):
-        src = mod4(y + d)
-        slot = gram_xy.at[src]
-        remote(slot, slot, gy_s.at[0], gy_r.at[src], p.dev(x, src, z, c)).wait_recv()
+    exch_gather.hand_on(NEAR)
+    for d, e in plane:
+        src_x, src_y = mod4(x + d), mod4(y + e)
+        slot = gram_xy.at[src_y, src_x]
+        remote(
+            slot, slot, gp_s.at[0], gp_r.at[4 * src_y + src_x], p.dev(src_x, src_y, z, c)
+        ).wait_recv()
 
     for i in range(32):
         n_x, n_lo, n_c, n_g = i // 8, (i // 4) % 2, (i // 2) % 2, i % 2
         gram_full[4 * i : 4 * i + 4, :] = gram_xy[2 * n_g + n_lo, n_x, 4 * n_c : 4 * n_c + 4, :]
     gram = gram_full[...]
-    gram_full[...] = inverse_factor(0.5 * (gram + gram.T))
+    gram_full[...] = inverse_factor(
+        0.5 * (gram + gram.T), lambda: exch_gather.hand_on(LATE)
+    )
     inverse = gram_full[pl.ds(pl.multiple_of(8 * p.b, 8), 8), :]
 
     for s in range(16):
@@ -672,10 +771,12 @@
         def _():
             occ_out(r).wait_send()
 
+    for_table(c, lambda i: table_copy(i).wait_send())
+    for_table(c, lambda i: table_on(i).wait_send())
     for d in range(1, NZ):
-        table_copy(d).wait_send()
         for h in range(2):
             resp_copy(h, d).wait_send()
+        for h in range(3):
             rs_copy(h, d).wait_send()
     for h in range(2):
         sib_resp(h).wait_send()
@@ -683,23 +784,32 @@
         halo_copy(h).wait_send()
     for i in range(len(z_line)):
         gram_copy(i).wait_send()
-    for d in (1, 2, 3):
-        gx_copy(d).wait_send()
-        gy_copy(d).wait_send()
+    for i in range(len(plane)):
+        gram_plane(i).wait_send()
     for gather in (occ_gather, resp_gather, exch_gather):
         gather.finish()
 
 
 def on_device(*arguments):
+    arguments = arguments[:7] + (arguments[7].T,)
     table = cosine_table(N)
     vmem = pl.BlockSpec(memory_space=pltpu.VMEM)
-    smem = pl.BlockSpec(memory_space=pltpu.SMEM)
+    hbm = pl.BlockSpec(memory_space=pltpu.HBM)
     dma = lambda n: pltpu.SemaphoreType.DMA((n,))
     scratch = [
-        pltpu.VMEM((4, SLAB, N), F32),
-        pltpu.VMEM((4, SLAB, N), F32),
-        pltpu.VMEM((2, NZ, 2 * SLAB, N), BF16),
-        pltpu.VMEM((4, 2 * SLAB, N), BF16),
+        pltpu.VMEM((4, SLAB, N), BF16),
+        pltpu.VMEM((8, SLAB, N), BF16),
+        pltpu.VMEM((8, SLAB, N), BF16),
+        pltpu.SMEM((8,), jnp.int32),
+        pltpu.SMEM((8,), F32),
+        pltpu.VMEM((SLAB, N), F32),
+        pltpu.VMEM((3, SLAB, N), F32),
+        pltpu.VMEM((N, N), BF16),
+        pltpu.VMEM((N, N), BF16),
+        pltpu.VMEM((4, WIRE_ONE, 128), BF16),
+        pltpu.VMEM((4, WIRE_ONE, 128), BF16),
+        pltpu.VMEM((2, NZ, WIRE, 128), BF16),
+        pltpu.VMEM((4, WIRE, 128), BF16),
         pltpu.VMEM((4, N, N), BF16),
         pltpu.VMEM((NZ, SLAB, N), F32),
         pltpu.VMEM((N, N), F32),
@@ -708,19 +818,21 @@
         pltpu.VMEM((16, 2, HALF, N), BF16),
         pltpu.VMEM((16, 2, HALF, N), BF16),
         pltpu.VMEM((16, 2, HALF, N), BF16),
-        pltpu.VMEM((2, N, N), F32),
-        pltpu.VMEM((2, NZ, 2 * SLAB, N), BF16),
-        pltpu.VMEM((2, NZ, 2 * SLAB, N), BF16),
+        pltpu.VMEM((4, N, N), F32),
+        pltpu.VMEM((NZ, WIRE, 128), BF16),
+        pltpu.VMEM((NZ, WIRE, 128), BF16),
+        pltpu.VMEM((2, NZ, WIRE_ONE, 128), BF16),
+        pltpu.VMEM((2, NZ, WIRE_ONE, 128), BF16),
         pltpu.VMEM((SLAB, 8, N), F32),
         pltpu.VMEM((4, SLAB, N), F32),
-        pltpu.VMEM((2, 2 * SLAB, N), BF16),
+        pltpu.VMEM((2, WIRE, 128), BF16),
         pltpu.VMEM((2 * NZ, 8, BANDS), F32),
         pltpu.VMEM((4, 4, 8, BANDS), F32),
         pltpu.VMEM((BANDS, BANDS), F32),
         pltpu.VMEM((256, BANDS), BF16),
         pltpu.VMEM((8, SLAB, N), F32),
     ]
-    counts = [4, 4, 14, 16, 4, 4, 7, 8, 2, 2, 14, 16, 15, 16, 3, 4, 3, 4] + [3, 12, 16, 16, 16] * 3
+    counts = [10, 4, 4, 14, 16, 4, 4, 4, 8, 4, 8, 2, 2, 21, 24, 15, 16, 15, 16] + [3, 12, 16, 16, 16] * 3
     scratch += [dma(n) for n in counts]
     return pl.pallas_call(
         kernel,
@@ -728,11 +840,11 @@
             jax.ShapeDtypeStruct((8, SLAB, N), BF16),
             jax.ShapeDtypeStruct((8, SLAB, N), F32),
         ),
-        in_specs=[vmem, vmem, vmem, smem, smem, vmem, vmem, vmem, vmem, vmem],
+        in_specs=[hbm] * 10,
         out_specs=(vmem, vmem),
         scratch_shapes=scratch,
         compiler_params=pltpu.CompilerParams(
-            collective_id=0, has_side_effects=True, vmem_limit_bytes=48 << 20
+            collective_id=0, has_side_effects=True, vmem_limit_bytes=64 << 20
         ),
         cost_estimate=pl.CostEstimate(
             flops=4 * 64 * 2 * N**3, bytes_accessed=4 << 20, transcendentals=0

time: 76.7 us -> 63 us (0.82)
  Pallas kernels: 67.4 us -> 59.9 us
  local copies, waits for them, and re-layouts: 7.89 us -> 2.26 us
    pallas_call x1, Pallas kernels: 67.4 us -> 59.9 us  [on_device(): pl.pallas_call(kernel, out_shape=(jax.ShapeDtypeStruct((8, SLAB, N), BF16...]
    unnamed x21 -> x4, local copies, waits for them, and re-layouts: 7.89 us -> 2.26 us
where the time goes in v2:
time: 63 us; the launch traced here: 62.8 us
  Pallas kernels  59.9 us (95%)
  local copies, waits for them, and re-layouts  2.26 us (4%)
  between operations  0.65 us (1%)
    pallas_call x1, Pallas kernels, on_device(): pl.pallas_call(kernel, out_shape=(jax.ShapeDtypeStruct((8, SLAB, N), BF16...  59.9 us
    unnamed x4, local copies, waits for them, and re-layouts  2.26 us

profile of v2, /device:TPU:1, one launch (start us, length us, event | category | flops | bytes accessed | tf_op | source)
XLA Modules:
  0.0 62.8 jit_solution(2419489794280445761)
XLA Ops:
  0.6 59.9 %shard_map.113 = (bf16[8,24,192]{2,1,0:T(8,128)(2,1)}, f32[8,24,192]{2,1,0:T(8,128)}) custom-call(bf16[4,24,192]{2,1,0:T(8,128)(2,1)} %occ_hbm.1, bf16[8,24,192]{2,1,0:T(8,128)(2,1)} %resp_hbm.1, bf16[8,24,192]{2,1,0:T(8,128)(2,1)} %ground_hbm.1, s32[8]{0:T(128)} %index_hbm.1, f32[8]{0:T(128)} %energy_hbm.1, f32[24,192]{1,0:T(8,128)} %local_hbm.1, ...), custom_call_target="tpu_custom_call" | custom-call | flops 3623878656 | bytes 4194304 | tf_op jit(solution)/shard_map/pallas_call | solution.py:837
  60.6 0.0 copy-start
  60.6 1.6 %copy.14 = bf16[8,24,192]{2,1,0:T(8,128)(2,1)} copy(bf16[8,24,192]{2,1,0:T(8,128)(2,1)} %get-tuple-element.4) | data formatting | bytes 147456
  62.2 0.0 copy-done
  62.2 0.7 %copy.15 = f32[8,24,192]{2,1,0:T(8,128)} copy(f32[8,24,192]{2,1,0:T(8,128)S(1)} %copy-done) | data formatting | bytes 294912
Async XLA Ops:
  60.6 1.6 %copy-start = (f32[8,24,192]{2,1,0:T(8,128)S(1)}, f32[8,24,192]{2,1,0:T(8,128)}, u32[]{:S(2)}) copy-start(f32[8,24,192]{2,1,0:T(8,128)} %get-tuple-element.5) | copy-start | bytes 442372

commit v3 on v2

--- a/solution.py
+++ b/solution.py
@@ -26,6 +26,15 @@
     factor = np.where(rows == 0, one, two).astype(np.float32)
     angle = np.float32(np.pi) * (cols + np.float32(0.5)) * rows / np.float32(length)
     return (factor * np.cos(angle)).astype(ml_dtypes.bfloat16)
+
+
+def split_wires(first, second):
+    first, second = first[: 3 * SLAB], second[: 3 * SLAB]
+    return jnp.concatenate([first, second[:8]], axis=0), second[8:]
+
+
+def join_wires(long, short):
+    return jnp.concatenate([long[3 * SLAB :], short], axis=0)
 
 
 def pack_one(slab):
@@ -46,6 +55,17 @@
     ends = value[SLAB : SLAB + 16]
     ends = jnp.concatenate([ends[:8, :64], ends[:8, 64:], ends[8:, :64]], axis=0)
     return [jnp.concatenate([value[:SLAB], ends], axis=1)]
+
+
+def pack_half(half):
+    ends = jnp.concatenate([half[: HALF // 2, 128:], half[HALF // 2 :, 128:]], axis=1)
+    return jnp.concatenate([half[:, :128], ends], axis=0).astype(BF16)
+
+
+def unpack_half(wire):
+    value = wire.astype(F32)
+    ends = jnp.concatenate([value[HALF:, :64], value[HALF:, 64:]], axis=0)
+    return jnp.concatenate([value[:HALF], ends], axis=1)
 
 
 def tree_sum(terms):
@@ -230,6 +250,7 @@
 
 Z_ORDER = (4, 3, 5, 2, 6, 1, 7)
 NEAR = ((0, 1), (0, 3), (0, 2))
+CROSS = ((0, 0), (1, 0), (0, 1), (3, 0), (0, 3), (2, 0), (0, 2))
 LATE = ((1, 1), (1, 3), (3, 1), (3, 3), (1, 2), (2, 1), (3, 2), (2, 3), (2, 2))
 WIRE_ONE = 48
 WIRE = 80
@@ -274,21 +295,23 @@
     ct_ref,
     occ_src,
     occ_got,
-    resp_got,
-    resp_sib,
+    resp_long,
+    resp_short,
+    sib_long,
+    sib_short,
+    exch_sib,
     resp_full,
     table_got,
     table,
     halo_src,
     halo_got,
     occ_all,
+    occ_full,
     resp_all,
     exch_all,
     total,
     rs_src,
     rs_got,
-    rs_src_one,
-    rs_got_one,
     rows32,
     exch_own,
     exch_wire,
@@ -308,7 +331,7 @@
     resp_s, resp_r = take(), take()
     sib_s, sib_r = take(), take()
     table_s, table_r = take(), take()
-    table_sib_s, table_sib_r = take(), take()
+    table_sib_s = take()
     halo_s, halo_r = take(), take()
     rs_s, rs_r = take(), take()
     gz_s, gz_r = take(), take()
@@ -339,7 +362,7 @@
 
     barrier = pltpu.get_barrier_semaphore()
     peers = [p.z_peer(d, k) for d in range(1, NZ) for k in (0, 1)]
-    peers += [p.sibling]
+    peers += [p.sibling, p.dev(x, p.y + 1 - 2 * p.y_lo, z, 1 - c)]
     plane = [(d, e) for d in (2, 1, 3, 0) for e in (2, 1, 3, 0) if (d, e) != (0, 0)]
     peers += [p.dev(mod4(x + d), mod4(y + e), z, c) for d, e in plane]
     for peer in peers:
@@ -349,9 +372,12 @@
         load.wait()
     for r in range(4):
         occ_src[r] = pack_one(occ_ref[r].astype(F32))
+    wires = []
     for h in range(2):
         pair = [resp_ref[4 * g + 2 * h + r].astype(F32) for r in range(2)]
-        resp_got[h, z] = pack(jnp.concatenate(pair, axis=0))
+        wires.append(pack(jnp.concatenate(pair, axis=0)).astype(F32))
+    for ref, wire in zip((resp_long, resp_short), split_wires(*wires)):
+        ref[z] = wire.astype(BF16)
     edge = [resp_ref[j].astype(F32) for j in range(8)]
     halo_src[0] = jnp.concatenate([e[SLAB - 1 : SLAB] for e in edge], axis=0)
     halo_src[1] = jnp.concatenate([e[0:1] for e in edge], axis=0)
@@ -390,64 +416,76 @@
         def _():
             occ_got[r] = occ_src[r]
 
+    k_table = 2 * p.y_lo + c
+    twin = p.y + 1 - 2 * p.y_lo
+    mates = [p.sibling, p.dev(x, twin, z, c), p.dev(x, twin, z, 1 - c)]
+
+    def table_slot(d):
+        src = lax.rem(z + NZ - d, NZ)
+        return table_got.at[src], table_r.at[src]
+
     def table_copy(i):
-        d = 2 * i + 2 - c
+        d = k_table + 4 * i
+        slot, recv = table_got.at[z], table_r.at[z]
+        return remote(slot, slot, table_s.at[i], recv, p.z_peer(d, c))
+
+    def table_on(i, m):
+        slot, recv = table_slot(k_table + 4 * i)
+        return remote(slot, slot, table_sib_s.at[3 * i + m], recv, mates[m])
+
+    def table_wait(i):
+        slot, recv = table_slot(k_table + 4 * i)
+        remote(slot, slot, table_s.at[0], recv, p.sibling).wait_recv()
+        for m in range(3):
+            table_on(i, m).start()
+
+    def table_wait_mates():
+        for m in range(1, 4):
+            other = lax.rem(k_table + m, 4)
+
+            @pl.when(other > 0)
+            def _():
+                slot, recv = table_slot(other)
+                remote(slot, slot, table_s.at[0], recv, p.sibling).wait_recv()
+
+            slot, recv = table_slot(other + 4)
+            remote(slot, slot, table_s.at[0], recv, p.sibling).wait_recv()
+
+    def for_table(act):
+        @pl.when(k_table > 0)
+        def _():
+            act(0)
+
+        act(1)
+
+    resp_got = (resp_long, resp_short)
+
+    def resp_copy(h, d):
+        slot = resp_got[h].at[z]
         return remote(
-            table_got.at[z], table_got.at[z], table_s.at[i], table_r.at[z], p.z_peer(d, c)
-        )
-
-    def table_on(i):
-        src = lax.rem(z + NZ - (2 * i + 2 - c), NZ)
-        slot = table_got.at[src]
-        return remote(slot, slot, table_sib_s.at[i], table_sib_r.at[src], p.sibling)
-
-    def table_wait(i):
-        src = lax.rem(z + NZ - (2 * i + 2 - c), NZ)
-        slot = table_got.at[src]
-        remote(slot, slot, table_s.at[0], table_r.at[src], p.sibling).wait_recv()
-        table_on(i).start()
-
-    def table_wait_sib(i):
-        src = lax.rem(z + NZ - (2 * i + 1 + c), NZ)
-        slot = table_got.at[src]
-        remote(slot, slot, table_sib_s.at[0], table_sib_r.at[src], p.sibling).wait_recv()
-
-    def for_table(core, act):
-        for i in range(3):
-            act(i)
-
-        @pl.when(core == 1)
-        def _():
-            act(3)
-
-    def resp_copy(h, d):
-        return remote(
-            resp_got.at[h, z],
-            resp_got.at[h, z],
-            resp_s.at[7 * h + d - 1],
-            resp_r.at[8 * h + z],
-            p.z_peer(d, c),
+            slot, slot, resp_s.at[7 * h + d - 1], resp_r.at[8 * h + z], p.z_peer(d, c)
         )
 
     def resp_wait(h, d):
         src = lax.rem(z + d, NZ)
-        remote(
-            resp_got.at[h, src],
-            resp_got.at[h, src],
-            resp_s.at[0],
-            resp_r.at[8 * h + src],
-            p.z_peer(d, c),
-        ).wait_recv()
+        slot = resp_got[h].at[src]
+        remote(slot, slot, resp_s.at[0], resp_r.at[8 * h + src], p.z_peer(d, c)).wait_recv()
 
     def sib_resp(h):
-        return remote(resp_got.at[h, z], resp_sib.at[h], sib_s.at[h], sib_r.at[h], p.sibling)
+        return remote(
+            resp_got[h].at[z], (sib_long, sib_short)[h], sib_s.at[h], sib_r.at[h], p.sibling
+        )
+
+    def two_pairs(long, short):
+        long, short = long.astype(F32), short.astype(F32)
+        return unpack(long) + unpack(join_wires(long, short))
 
     def halo_copy(k):
         return remote(
             halo_src.at[k], halo_got.at[k], halo_s.at[k], halo_r.at[k], p.z_peer((1, 7)[k], c)
         )
 
-    for_table(c, lambda i: table_copy(i).start())
+    for_table(lambda i: table_copy(i).start())
     for d in Z_ORDER:
         resp_copy(0, d).start()
     for d in Z_ORDER:
@@ -463,9 +501,9 @@
             occ_in(q).wait_recv()
 
     own = 4 * y + x
-    occ_all[own, c] = jnp.concatenate(
-        [unpack_one(occ_got[q])[0] for q in range(4)], axis=0
-    ).astype(BF16)
+    occ_all[own, c] = pack_half(
+        jnp.concatenate([unpack_one(occ_got[q])[0] for q in range(4)], axis=0)
+    )
     occ_gather.start()
 
     def arrange(parts):
@@ -488,46 +526,53 @@
 
     for h in range(2):
         sib_resp(h).wait_recv()
-    arrange(by_core(slab_of(lambda h: resp_got[h, z]), slab_of(lambda h: resp_sib[h])))
+    ours = two_pairs(resp_long[z], resp_short[z])
+    theirs = two_pairs(sib_long[...], sib_short[...])
+    arrange(by_core(lambda r: ours[r], lambda r: theirs[r]))
     resp_all[own, c] = rows_half()
 
     for load in loads[3:]:
         load.wait()
-    for_table(c, table_wait)
+    for_table(table_wait)
     occ_gather.forward()
     occ_gather.hand_on(NEAR)
-    for_table(1 - c, table_wait_sib)
+    table_wait_mates()
     table[...] = table_got[...].reshape(N, N).T
 
     def whole_bands(h):
         for d in Z_ORDER:
             resp_wait(h, d)
-        parts = [unpack(resp_got[h, s]) for s in range(NZ)]
+        if h == 0:
+            parts = [unpack(resp_long[s]) for s in range(NZ)]
+        else:
+            parts = [two_pairs(resp_long[s], resp_short[s])[2:] for s in range(NZ)]
         for r in range(2):
             whole = [parts[s][r] for s in range(NZ)]
             resp_full[2 * h + r] = jnp.concatenate(whole, axis=0).astype(BF16)
 
     whole_bands(0)
 
-    def pick(t, values):
-        out = values[0]
-        for i in range(1, 4):
-            out = jnp.where(t == i, values[i], out)
+    def slot_at(dx, dy):
+        return 4 * mod4(y + dy) + mod4(x + dx)
+
+    def receive(sl):
+        occ_gather.wait_sib(sl)
+        halves = [unpack_half(occ_all[sl, k]) for k in range(2)]
+        occ_full[sl] = jnp.concatenate(halves, axis=0).astype(BF16)
+
+    def late_slots(t):
+        out = []
+        for q in range(3):
+            pick = [LATE[3 * i + q] for i in range(3)]
+            dx, dy = [
+                jnp.where(t == 0, pick[0][k], jnp.where(t == 1, pick[1][k], pick[2][k]))
+                for k in range(2)
+            ]
+            out.append(slot_at(dx, dy))
         return out
 
-    STEPS_X = ((0, 1, 0, 3), (0, 2, 0, 1), (1, 3, 3, 1), (2, 3, 2, 2))
-    STEPS_Y = ((0, 0, 1, 0), (3, 0, 2, 1), (3, 1, 3, 2), (1, 2, 3, 2))
-
-    def slots_of(t):
-        out = []
-        for q in range(4):
-            dx = pick(t, [STEPS_X[i][q] for i in range(4)])
-            dy = pick(t, [STEPS_Y[i][q] for i in range(4)])
-            out.append(4 * mod4(y + dy) + mod4(x + dx))
-        return out
-
     def pairs(slots, bands):
-        orbitals = [occ_all[sl].reshape(N, N) for sl in slots]
+        orbitals = [occ_full[sl] for sl in slots]
         which = [(r, q) for r in bands for q in range(len(slots))]
         first = [
             jnp.dot(orbitals[q] * resp_full[r], ct_ref[...], preferred_element_type=F32).astype(BF16)
@@ -543,86 +588,84 @@
         for r in bands:
             acc = total[r]
             for i, (band, q) in enumerate(which):
-                if band == r:
+                if band is r:
                     potential = jnp.dot(third[i], c_ref[...], preferred_element_type=F32)
                     acc = acc + orbitals[q].astype(F32) * potential
             total[r] = acc
 
-    groups = ((0, 1), (2,), (3,))
-
-    def rs_refs(h):
-        if h == 0:
-            return rs_src, rs_got
-        return rs_src_one.at[h - 1], rs_got_one.at[h - 1]
-
     def rs_copy(h, d):
         to = lax.rem(z + d, NZ)
-        src, dst = rs_refs(h)
         return remote(
-            src.at[to], dst.at[z], rs_s.at[7 * h + d - 1], rs_r.at[8 * h + z], p.z_peer(d, c)
+            rs_src.at[h, to],
+            rs_got.at[h, z],
+            rs_s.at[7 * h + d - 1],
+            rs_r.at[8 * h + z],
+            p.z_peer(d, c),
         )
 
     def reduce_start(h):
-        src, _ = rs_refs(h)
+        bands = (2 * h, 2 * h + 1)
         for s in range(NZ):
-            out = [total[r, SLAB * s : SLAB * s + SLAB, :] * (1.0 / BANDS) for r in groups[h]]
-            src[s] = pack(jnp.concatenate(out, axis=0)) if h == 0 else pack_one(out[0])
+            out = [total[r, SLAB * s : SLAB * s + SLAB, :] * (1.0 / BANDS) for r in bands]
+            rs_src[h, s] = pack(jnp.concatenate(out, axis=0))
         for d in Z_ORDER:
             rs_copy(h, d).start()
         start = pl.multiple_of(SLAB * z, 8)
-        for r in groups[h]:
+        for r in bands:
             exch_own[r] = total[r, pl.ds(start, SLAB), :] * (1.0 / BANDS)
 
     def reduce_finish(h):
-        _, dst = rs_refs(h)
-        acc = [exch_own[r] for r in groups[h]]
+        bands = (2 * h, 2 * h + 1)
+        acc = [exch_own[r] for r in bands]
         for d in Z_ORDER:
             src = lax.rem(z + d, NZ)
-            slot = dst.at[src]
+            slot = rs_got.at[h, src]
             remote(slot, slot, rs_s.at[0], rs_r.at[8 * h + src], p.z_peer(d, c)).wait_recv()
-            got = unpack(dst[src]) if h == 0 else unpack_one(dst[src])
-            acc = [a + b for a, b in zip(acc, got)]
-        for r, a in zip(groups[h], acc):
+            acc = [a + b for a, b in zip(acc, unpack(rs_got[h, src]))]
+        for r, a in zip(bands, acc):
             exch_own[r] = a
 
     total[...] = jnp.zeros_like(total)
-
-    def step_one(t, carry):
-        @pl.when(t == 3)
+    near = [slot_at(dx, dy) for dx, dy in CROSS]
+    for sl in near:
+        receive(sl)
+
+    def near_step(h, carry):
+        @pl.when(h == 1)
         def _():
-            resp_gather.start()
-
-        for sl in slots_of(t):
-            occ_gather.wait_sib(sl)
-        pairs(slots_of(t), groups[0])
-
-        @pl.when(t == 0)
+            occ_gather.hand_on(LATE[:3])
+
+        for some in (near[:4], near[4:]):
+            pairs(some, (2 * h, 2 * h + 1))
+        return carry
+
+    whole_bands(1)
+    lax.fori_loop(0, 2, near_step, 0)
+    occ_gather.hand_on(LATE[3:])
+    resp_gather.start()
+
+    def late_step(i, carry):
+        h, t = lax.div(i, 3), lax.rem(i, 3)
+
+        @pl.when(h == 0)
         def _():
-            occ_gather.hand_on(LATE[:4])
-
-        @pl.when(t == 1)
+            for sl in late_slots(t):
+                receive(sl)
+
+        pairs(late_slots(t), (2 * h, 2 * h + 1))
+
+        @pl.when(t == 2)
         def _():
-            occ_gather.hand_on(LATE[4:])
+            reduce_start(h)
+
+        @pl.when(i == 4)
+        def _():
+            resp_gather.forward()
+            resp_gather.hand_on(NEAR)
 
         return carry
 
-    lax.fori_loop(0, 4, step_one, 0)
-    reduce_start(0)
-    whole_bands(1)
-
-    def later_step(bands):
-        def step(t, carry):
-            pairs([8 * t + q for q in range(8)], bands)
-            return carry
-
-        return step
-
-    lax.fori_loop(0, 2, later_step(groups[1]), 0)
-    reduce_start(1)
-    resp_gather.forward()
-    resp_gather.hand_on(NEAR)
-    lax.fori_loop(0, 2, later_step(groups[2]), 0)
-    reduce_start(2)
+    lax.fori_loop(0, 6, late_step, 0)
 
     resp_gather.hand_on(LATE)
     for k in range(2):
@@ -649,11 +692,26 @@
     spread[...] = jnp.where(natural == col, 1.0, 0.0).astype(BF16)
     parity = (lax.broadcasted_iota(jnp.int32, (8, 256), 1) // 8) % 2
 
+    for r in range(4):
+        @pl.when(jnp.logical_not(mine(r)))
+        def _():
+            occ_out(r).wait_send()
+
+    for_table(lambda i: table_copy(i).wait_send())
+    for m in range(3):
+        for_table(lambda i: table_on(i, m).wait_send())
+    for h in range(2):
+        for d in range(1, NZ):
+            resp_copy(h, d).wait_send()
+        sib_resp(h).wait_send()
+        halo_copy(h).wait_send()
+    occ_gather.finish()
+
     for s in range(16):
         resp_gather.wait_sib(s)
 
     def sib_exch(h):
-        return remote(exch_wire.at[h], resp_sib.at[2 + h], sib_s.at[2 + h], sib_r.at[2 + h], p.sibling)
+        return remote(exch_wire.at[h], exch_sib.at[h], sib_s.at[2 + h], sib_r.at[2 + h], p.sibling)
 
     def sib_exch_start(h):
         exch_wire[h] = pack(jnp.concatenate([exch_own[2 * h], exch_own[2 * h + 1]], axis=0))
@@ -662,7 +720,6 @@
     reduce_finish(0)
     sib_exch_start(0)
     reduce_finish(1)
-    reduce_finish(2)
     sib_exch_start(1)
 
     zero = jnp.zeros((SLAB, N), F32)
@@ -700,9 +757,15 @@
 
     for h in range(2):
         sib_exch(h).wait_recv()
-    arrange(by_core(own_part, slab_of(lambda h: resp_sib[2 + h])))
+    arrange(by_core(own_part, slab_of(lambda h: exch_sib[h])))
     exch_all[own, c] = rows_half()
     exch_gather.start()
+
+    resp_gather.finish()
+    for h in range(2):
+        sib_exch(h).wait_send()
+        for d in range(1, NZ):
+            rs_copy(h, d).wait_send()
 
     for d, k in z_line:
         src = 2 * lax.rem(z + d, NZ) + line_core(k)
@@ -723,6 +786,8 @@
         gram_plane(i).start()
     exch_gather.forward()
     exch_gather.hand_on(NEAR)
+    for i in range(len(z_line)):
+        gram_copy(i).wait_send()
     for d, e in plane:
         src_x, src_y = mod4(x + d), mod4(y + e)
         slot = gram_xy.at[src_y, src_x]
@@ -766,28 +831,9 @@
     for j in range(8):
         proj_ref[j] = proj32[j].astype(BF16)
 
-    for r in range(4):
-        @pl.when(jnp.logical_not(mine(r)))
-        def _():
-            occ_out(r).wait_send()
-
-    for_table(c, lambda i: table_copy(i).wait_send())
-    for_table(c, lambda i: table_on(i).wait_send())
-    for d in range(1, NZ):
-        for h in range(2):
-            resp_copy(h, d).wait_send()
-        for h in range(3):
-            rs_copy(h, d).wait_send()
-    for h in range(2):
-        sib_resp(h).wait_send()
-        sib_exch(h).wait_send()
-        halo_copy(h).wait_send()
-    for i in range(len(z_line)):
-        gram_copy(i).wait_send()
     for i in range(len(plane)):
         gram_plane(i).wait_send()
-    for gather in (occ_gather, resp_gather, exch_gather):
-        gather.finish()
+    exch_gather.finish()
 
 
 def on_device(*arguments):
@@ -808,21 +854,23 @@
         pltpu.VMEM((N, N), BF16),
         pltpu.VMEM((4, WIRE_ONE, 128), BF16),
         pltpu.VMEM((4, WIRE_ONE, 128), BF16),
-        pltpu.VMEM((2, NZ, WIRE, 128), BF16),
-        pltpu.VMEM((4, WIRE, 128), BF16),
+        pltpu.VMEM((NZ, WIRE, 128), BF16),
+        pltpu.VMEM((NZ, WIRE - 16, 128), BF16),
+        pltpu.VMEM((WIRE, 128), BF16),
+        pltpu.VMEM((WIRE - 16, 128), BF16),
+        pltpu.VMEM((2, WIRE, 128), BF16),
         pltpu.VMEM((4, N, N), BF16),
         pltpu.VMEM((NZ, SLAB, N), F32),
         pltpu.VMEM((N, N), F32),
         pltpu.VMEM((2, 8, N), F32),
         pltpu.VMEM((2, 8, N), F32),
-        pltpu.VMEM((16, 2, HALF, N), BF16),
+        pltpu.VMEM((16, 2, 3 * HALF // 2, 128), BF16),
+        pltpu.VMEM((16, N, N), BF16),
         pltpu.VMEM((16, 2, HALF, N), BF16),
         pltpu.VMEM((16, 2, HALF, N), BF16),
         pltpu.VMEM((4, N, N), F32),
-        pltpu.VMEM((NZ, WIRE, 128), BF16),
-        pltpu.VMEM((NZ, WIRE, 128), BF16),
-        pltpu.VMEM((2, NZ, WIRE_ONE, 128), BF16),
-        pltpu.VMEM((2, NZ, WIRE_ONE, 128), BF16),
+        pltpu.VMEM((2, NZ, WIRE, 128), BF16),
+        pltpu.VMEM((2, NZ, WIRE, 128), BF16),
         pltpu.VMEM((SLAB, 8, N), F32),
         pltpu.VMEM((4, SLAB, N), F32),
         pltpu.VMEM((2, WIRE, 128), BF16),
@@ -832,19 +880,16 @@
         pltpu.VMEM((256, BANDS), BF16),
         pltpu.VMEM((8, SLAB, N), F32),
     ]
-    counts = [10, 4, 4, 14, 16, 4, 4, 4, 8, 4, 8, 2, 2, 21, 24, 15, 16, 15, 16] + [3, 12, 16, 16, 16] * 3
+    counts = [10, 4, 4, 14, 16, 4, 4, 2, 8, 6, 2, 2, 14, 16, 15, 16, 15, 16] + [3, 12, 16, 16, 16] * 3
     scratch += [dma(n) for n in counts]
     return pl.pallas_call(
         kernel,
-        out_shape=(
-            jax.ShapeDtypeStruct((8, SLAB, N), BF16),
-            jax.ShapeDtypeStruct((8, SLAB, N), F32),
-        ),
+        out_shape=(pltpu.VMEM((8, SLAB, N), BF16), pltpu.VMEM((8, SLAB, N), F32)),
         in_specs=[hbm] * 10,
         out_specs=(vmem, vmem),
         scratch_shapes=scratch,
         compiler_params=pltpu.CompilerParams(
-            collective_id=0, has_side_effects=True, vmem_limit_bytes=64 << 20
+            collective_id=0, has_side_effects=True, vmem_limit_bytes=(64 << 20) - (10500 << 10)
         ),
         cost_estimate=pl.CostEstimate(
             flops=4 * 64 * 2 * N**3, bytes_accessed=4 << 20, transcendentals=0

time: 63 us -> 62.1 us (0.986)
  local copies, waits for them, and re-layouts: 2.26 us -> 1.32 us
    unnamed x4 -> x2, local copies, waits for them, and re-layouts: 2.26 us -> 1.32 us
where the time goes in v3:
time: 62.1 us; the launch traced here: 62 us
  Pallas kernels  60 us (97%)
  local copies, waits for them, and re-layouts  1.32 us (2%)
  between operations  0.64 us (1%)
    pallas_call x1, Pallas kernels, on_device(): pl.pallas_call(kernel, out_shape=(pltpu.VMEM((8, SLAB, N), BF16), pltpu.V...  60 us
    unnamed x2, local copies, waits for them, and re-layouts  1.32 us

profile of v3, /device:TPU:1, one launch (start us, length us, event | category | flops | bytes accessed | tf_op | source)
XLA Modules:
  0.0 62.0 jit_solution(15745889156290370647)
XLA Ops:
  0.6 60.0 %shard_map.113 = (bf16[8,24,192]{2,1,0:T(8,128)(2,1)S(1)}, f32[8,24,192]{2,1,0:T(8,128)S(1)}) custom-call(bf16[4,24,192]{2,1,0:T(8,128)(2,1)} %occ_hbm.1, bf16[8,24,192]{2,1,0:T(8,128)(2,1)} %resp_hbm.1, bf16[8,24,192]{2,1,0:T(8,128)(2,1)} %ground_hbm.1, s32[8]{0:T(128)} %index_hbm.1, f32[8]{0:T(128)} %energy_hbm.1, f32[24,192]{1,0:T(8,128)} %local_hbm.1, ...), custom_call_target="tpu_custom_call" | custom-call | flops 3623878656 | bytes 4194304 | tf_op jit(solution)/shard_map/pallas_call | solution.py:885
  60.7 0.6 %copy.14 = bf16[8,24,192]{2,1,0:T(8,128)(2,1)} copy(bf16[8,24,192]{2,1,0:T(8,128)(2,1)S(1)} %get-tuple-element.2) | data formatting | bytes 147456
  61.3 0.7 %copy.15 = f32[8,24,192]{2,1,0:T(8,128)} copy(f32[8,24,192]{2,1,0:T(8,128)S(1)} %get-tuple-element.3) | data formatting | bytes 294912

commit v4 on v3

--- a/solution.py
+++ b/solution.py
@@ -536,6 +536,7 @@
     for_table(table_wait)
     occ_gather.forward()
     occ_gather.hand_on(NEAR)
+    resp_gather.start()
     table_wait_mates()
     table[...] = table_got[...].reshape(N, N).T
 
@@ -642,7 +643,6 @@
     whole_bands(1)
     lax.fori_loop(0, 2, near_step, 0)
     occ_gather.hand_on(LATE[3:])
-    resp_gather.start()
 
     def late_step(i, carry):
         h, t = lax.div(i, 3), lax.rem(i, 3)
@@ -658,7 +658,7 @@
         def _():
             reduce_start(h)
 
-        @pl.when(i == 4)
+        @pl.when(i == 2)
         def _():
             resp_gather.forward()
             resp_gather.hand_on(NEAR)
@@ -799,9 +799,13 @@
         n_x, n_lo, n_c, n_g = i // 8, (i // 4) % 2, (i // 2) % 2, i % 2
         gram_full[4 * i : 4 * i + 4, :] = gram_xy[2 * n_g + n_lo, n_x, 4 * n_c : 4 * n_c + 4, :]
     gram = gram_full[...]
-    gram_full[...] = inverse_factor(
-        0.5 * (gram + gram.T), lambda: exch_gather.hand_on(LATE)
-    )
+
+    def halfway():
+        exch_gather.hand_on(LATE)
+        for i in range(len(plane)):
+            gram_plane(i).wait_send()
+
+    gram_full[...] = inverse_factor(0.5 * (gram + gram.T), halfway)
     inverse = gram_full[pl.ds(pl.multiple_of(8 * p.b, 8), 8), :]
 
     for s in range(16):
@@ -831,8 +835,6 @@
     for j in range(8):
         proj_ref[j] = proj32[j].astype(BF16)
 
-    for i in range(len(plane)):
-        gram_plane(i).wait_send()
     exch_gather.finish()
 
 

time: 62.1 us -> 61.1 us (0.984)
  Pallas kernels: 60 us -> 59.1 us
    pallas_call x1, Pallas kernels: 60 us -> 59.1 us  [on_device(): pl.pallas_call(kernel, out_shape=(pltpu.VMEM((8, SLAB, N), BF16), pltpu.V...]
where the time goes in v4:
time: 61.1 us; the launch traced here: 61 us
  Pallas kernels  59.1 us (97%)
  local copies, waits for them, and re-layouts  1.32 us (2%)
  between operations  0.64 us (1%)
    pallas_call x1, Pallas kernels, on_device(): pl.pallas_call(kernel, out_shape=(pltpu.VMEM((8, SLAB, N), BF16), pltpu.V...  59.1 us
    unnamed x2, local copies, waits for them, and re-layouts  1.32 us

profile of v4, /device:TPU:1, one launch (start us, length us, event | category | flops | bytes accessed | tf_op | source)
XLA Modules:
  0.0 61.0 jit_solution(12812490323396497259)
XLA Ops:
  0.6 59.1 %shard_map.113 = (bf16[8,24,192]{2,1,0:T(8,128)(2,1)S(1)}, f32[8,24,192]{2,1,0:T(8,128)S(1)}) custom-call(bf16[4,24,192]{2,1,0:T(8,128)(2,1)} %occ_hbm.1, bf16[8,24,192]{2,1,0:T(8,128)(2,1)} %resp_hbm.1, bf16[8,24,192]{2,1,0:T(8,128)(2,1)} %ground_hbm.1, s32[8]{0:T(128)} %index_hbm.1, f32[8]{0:T(128)} %energy_hbm.1, f32[24,192]{1,0:T(8,128)} %local_hbm.1, ...), custom_call_target="tpu_custom_call" | custom-call | flops 3623878656 | bytes 4194304 | tf_op jit(solution)/shard_map/pallas_call | solution.py:887
  59.7 0.6 %copy.14 = bf16[8,24,192]{2,1,0:T(8,128)(2,1)} copy(bf16[8,24,192]{2,1,0:T(8,128)(2,1)S(1)} %get-tuple-element.2) | data formatting | bytes 147456
  60.3 0.7 %copy.15 = f32[8,24,192]{2,1,0:T(8,128)} copy(f32[8,24,192]{2,1,0:T(8,128)S(1)} %get-tuple-element.3) | data formatting | bytes 294912
